TPU v7x, 32 devices: a whole 2x2x4 slice. The times are simulated.
32 devices in a mesh: parts: 2 (over y), tm: 4 (over z), axial: 2 (over x), chan: 2 (over core).
Axes of the slice: x: 2, y: 2, z: 4, core: 2. Of those that a mesh axis runs over, the one named last changes fastest.
Arguments:
- frames_in: bfloat16 [48, 8, 64, 128], P(('parts', 'tm'), 'axial'), parts along dimension 0, may hold values from -6 to 6
- spatial_weight: bfloat16 [6, 3, 64, 144], P('parts', None, None, 'chan'), parts along dimension 0, may hold values from -0.25 to 0.25
- temporal_weight: bfloat16 [6, 144, 64], P('parts', 'chan'), parts along dimension 0, may hold values from -0.3125 to 0.3125
- upstream: bfloat16 [48, 8, 64, 128], P(('parts', 'tm'), 'axial'), parts along dimension 0, may hold values from -6 to 6
Outputs:
- output: bfloat16 [48, 8, 64, 128], P(('parts', 'tm'), 'axial', 'chan'), parts along dimension 0
- input_grad: bfloat16 [48, 8, 64, 128], P(('parts', 'tm'), 'axial', 'chan'), parts along dimension 0
- spatial_grad: float32 [6, 3, 64, 144], P('parts', None, None, 'chan'), parts along dimension 0
- temporal_grad: float32 [6, 144, 64], P('parts', 'chan'), parts along dimension 0
There are 2 independent parts, one for each index of `parts`. A program takes and returns all parts, laid end to end along the dimension named above; each array names one. Nothing has to cross between parts.
All inputs are finite; a program needn't handle non-finite values.
Results may differ from a plain program's by a relative error of at most 0.009.
Values may be sent and summed in bfloat16 or wider, within the bound.
No kernel may reach another device: no remote copies, remote signals or barrier semaphores. Data moves between devices by JAX's collectives and lax.ppermute only.
A program may use at most 64 MiB of HBM per device.

v0:
```python
import functools
import math

import jax
import jax.numpy as jnp
from jax import lax
from jax.experimental import pallas as pl
from jax.experimental.pallas import tpu as pltpu
from jax.sharding import PartitionSpec as P

F32 = jnp.float32
BF16 = jnp.bfloat16
LANES = 128
HBM = pl.BlockSpec(memory_space=pltpu.HBM)
VMEM = pl.BlockSpec(memory_space=pltpu.VMEM)


def ring(count, step):
    return [(i, (i + step) % count) for i in range(count)]


def pairs(count, stride):
    return [(i, i ^ stride) for i in range(count)]


def facing(count):
    order = []
    for i in range(count):
        order += [(2 * i, 2 * ((i - 1) % count) + 1), (2 * i + 1, 2 * ((i + 1) % count))]
    return order


def dot(a, b):
    return jnp.dot(a, b, preferred_element_type=F32)


def dot_nt(a, b):
    return lax.dot_general(a, b, (((1,), (1,)), ((), ())), preferred_element_type=F32)


def moved(value, step):
    width = value.shape[1]
    column = lax.broadcasted_iota(jnp.int32, value.shape, 1)
    edge = 0 if step > 0 else width - 1
    return jnp.where(column == edge, 0.0, pltpu.roll(value, step % width, 1))


def pieces(depth, total):
    blocks, row = [], 0
    for first in range(0, total - total % LANES, LANES):
        blocks.append((row, 0, 0, first, depth, LANES))
        row += depth
    rest = total % LANES
    if rest:
        fold = LANES // rest
        if LANES % rest or depth % (8 * fold):
            fold = 1
        part = depth // fold
        for g in range(fold):
            blocks.append((row, g * rest, g * part, total - rest, part, rest))
        row += part
    return blocks, row


def padded(count):
    return -(-count // 16) * 16


def with_rows(value, count):
    if value.shape[0] == count:
        return value
    return jnp.concatenate([value, jnp.zeros((count - value.shape[0], value.shape[1]), value.dtype)], 0)


def half_rows(depth, total):
    return -(-pieces(depth, total)[1] // 32) * 16


def stage_kernel(split, x, u, sw, tw, edge, frame, sems):
    frames, rows = x.shape[:2]
    core = lax.axis_index("chan")
    if split:
        row = jnp.where(lax.axis_index("axial") == 0, rows - 1, 0)
        picked = pl.ds(core * (frames // 2), frames // 2)
    else:
        row = core * (rows - 1)
        picked = pl.ds(0, frames)
    copies = [
        pltpu.make_async_copy(u.at[core * (frames - 1)], frame, sems.at[0]),
        pltpu.make_async_copy(x.at[picked, row], edge, sems.at[1]),
    ]
    for copy in copies:
        copy.start()
    for copy in copies:
        copy.wait()


def prepare(sw, tw, wf, twf):
    channels, mid = tw.shape[1:]
    for j in range(3):
        wf[j * mid : (j + 1) * mid] = sw[:, j].reshape(3 * channels, mid).astype(F32).T
    twf[...] = jnp.concatenate([tw[k].astype(F32) for k in (2, 1, 0)], 0).T
    return wf[...].astype(BF16), twf[...].astype(BF16)


def activations(w_taps, w_act, field, cot, width):
    mid = w_act.shape[0]
    taps = dot(w_taps, field)
    act = dot(w_act, cot)
    hids, grads = [], []
    for first in range(0, field.shape[1], width):
        cols = slice(first, first + width)
        pre = taps[mid : 2 * mid, cols] + moved(taps[:mid, cols], 1) + moved(taps[2 * mid :, cols], -1)
        s = 0.5 * jnp.tanh(0.5 * pre) + 0.5
        hids.append(pre * s)
        grads.append(act[:, cols] * s * (1.0 + pre * (1.0 - s)))
    return hids, grads


def gathered(xp, up, h, picked):
    depth = 3 * xp.shape[2]
    width = xp.shape[3]
    field = jnp.concatenate([xp[f, pl.ds(h, 3)].reshape(depth, width) for f in picked], 1)
    cot = jnp.concatenate([jnp.concatenate([up[f + d, h] for d in range(3)], 0) for f in picked], 1)
    return field, cot


def inner_rows(axial_count, rows):
    if axial_count == 2:
        low = lax.axis_index("axial") == 0
        return jnp.where(low, 0, 1), rows - 1, [jnp.where(low, rows - 1, 0)]
    return 1, rows - 2, [0, rows - 1]


def cell_grads(xp, up, w_taps, w_act, groups, store):
    fields, cots, shifts, owns = [], [], [], []
    width = xp.shape[3]
    for h, picked in groups:
        field, cot = gathered(xp, up, h, picked)
        hids, grads = activations(w_taps, w_act, field, cot, width)
        shifts.append(
            jnp.concatenate(
                [
                    jnp.concatenate([moved(v, -1) for v in grads], 1),
                    jnp.concatenate(grads, 1),
                    jnp.concatenate([moved(v, 1) for v in grads], 1),
                ],
                0,
            ).astype(BF16)
        )
        hids = [with_rows(v, padded(v.shape[0])).astype(BF16) for v in hids]
        owns.append(jnp.concatenate(hids, 1))
        for f, hid, grad in zip(picked, hids, grads):
            store(h, f, hid, with_rows(grad, padded(grad.shape[0])).astype(BF16))
        fields.append(field)
        cots.append(cot)
    return (
        dot_nt(jnp.concatenate(fields, 1), jnp.concatenate(shifts, 1)),
        dot_nt(jnp.concatenate(cots, 1), jnp.concatenate(owns, 1))[:, : w_act.shape[0]],
    )


def inner_kernel(dims, *refs):
    frames, rows, channels, width, mid, own_c, rank_count, axial_count, group = dims
    x, u, sw, tw = refs[:4]
    hid_out, grad_out, acc_out, xp, up, taps_out, act_out, wf, twf = refs[4:]
    for f in range(frames):
        for at in (0, rows + 1):
            xp[f, at] = jnp.zeros((channels, width), BF16)
        for h in range(rows):
            xp[f, h + 1] = x[f, h]
            up[f + 1, h] = u[f, h]
    for at in (0, frames + 1):
        up[at] = jnp.zeros(up.shape[1:], BF16)
    w_taps, w_act = prepare(sw, tw, wf, twf)
    taps_out[...] = w_taps
    act_out[...] = w_act

    first, count, _ = inner_rows(axial_count, rows)

    def store(h, f, hid, grad):
        hid_out[h - first, f - 1] = hid
        grad_out[h - first, f - 1] = grad

    groups = [(first + i, (f, f + 1)) for i in range(count) for f in range(1, frames - 1, 2)]
    w_part, t_part = cell_grads(xp, up, w_taps, w_act, groups, store)
    acc_out[:, : 3 * mid] = w_part
    acc_out[:, 3 * mid :] = t_part


def grads_kernel(dims, *refs):
    frames, rows, channels, width, mid, own_c, rank_count, axial_count, group = dims
    hid_in, grad_in, acc_in, x, u, edge, frame, swapped, taps_in, act_in = refs[:10]
    hid_out, grad_out, xp, up, half_0, half_1, edges, acc, packed = refs[10:]
    axial = lax.axis_index("axial")
    core = lax.axis_index("chan")
    w_taps, w_act = taps_in[...], act_in[...]

    has_lo = (axial > 0).astype(BF16)
    has_hi = (axial < axial_count - 1).astype(BF16)
    part = edge.shape[0]
    edges[pl.ds(core * part, part)] = edge[...]
    edges[pl.ds((1 - core) * part, part)] = swapped[0:part]
    at_hi = 2 * part - frames
    for f in range(frames):
        xp[f, 0] = edges[f] * has_lo
        xp[f, rows + 1] = edges[at_hi + f] * has_hi
        for h in range(rows):
            xp[f, h + 1] = x[f, h + 1]
            up[f + 1, h] = u[f + 1, h]
    up[core * (frames + 1)] = frame[...]
    up[(1 - core) * (frames + 1)] = swapped[part:]

    first, count, others = inner_rows(axial_count, rows)

    def store(h, f, hid, grad):
        hid_out[h, f] = hid
        grad_out[h, f] = grad

    for i in range(count):
        for f in range(1, frames - 1):
            store(first + i, f, hid_in[i, f - 1], grad_in[i, f - 1])
    groups = [(first + i, (0, frames - 1)) for i in range(count)]
    groups += [(h, (f, f + 1)) for h in others for f in range(0, frames, 2)]
    w_part, t_part = cell_grads(xp, up, w_taps, w_act, groups, store)
    factor = 1.0 / math.sqrt(frames * rows * width * rank_count)
    acc[:, : 3 * mid] = (acc_in[:, : 3 * mid] + w_part) * factor
    acc[:, 3 * mid :] = (acc_in[:, 3 * mid :] + t_part) * factor

    blocks, used = pieces(*acc.shape)
    size = packed.shape[0] // 2
    packed[used:] = jnp.zeros((2 * size - used, LANES), F32)
    for at, lane, source, column, depth, total in blocks:
        packed[at : at + depth, lane : lane + total] = acc[source : source + depth, column : column + total]
    half_0[...] = packed[:size].astype(half_0.dtype)
    half_1[...] = packed[size:].astype(half_1.dtype)


def others_kernel(dims, *refs):
    frames, rows, channels, width, mid, own_c, rank_count, axial_count, group = dims
    xp, up, sw, tw, hid_out, grad_out, wf, twf = refs
    w_taps, w_act = prepare(sw, tw, wf, twf)
    for h in range(rows):
        for first in range(0, frames, group):
            picked = range(first, first + group)
            field, cot = gathered(xp, up, h, picked)
            for f, hid, grad in zip(picked, *activations(w_taps, w_act, field, cot, width)):
                hid_out[h, f] = with_rows(hid, padded(mid)).astype(BF16)
                grad_out[h, f] = with_rows(grad, padded(mid)).astype(BF16)


def fields_kernel(dims, fast, *refs):
    frames, rows, channels, width, mid, own_c, rank_count, axial_count, group = dims
    hid_in, grad_in, hid_other, grad_other, sw, tw, sw_other, tw_other = refs[:8]
    out, out_a, out_b, ig, ig_a, ig_b, twt, wg, ig_acc, out_edges = refs[8:]
    own = pl.ds(pl.multiple_of(lax.axis_index("chan") * own_c, own_c), own_c)
    blank = jnp.zeros((own_c, padded(mid) - mid), F32)

    def both(a, b):
        return jnp.concatenate([a.astype(F32), blank, b.astype(F32), blank], 1).astype(BF16)

    for k in range(3):
        twt[k * own_c : (k + 1) * own_c] = both(tw[k, own], tw_other[k, own])
    for i in range(3):
        for j in range(3):
            at = (i * 3 + j) * own_c
            wg[at : at + own_c] = both(sw[i, j, own], sw_other[i, j, own])
    w_out, w_in = twt[...], wg[...]

    for h in range(rows):
        out_terms = {}
        for first in range(0, frames, group):
            picked = range(first, first + group)
            hid = jnp.concatenate([jnp.concatenate([hid_in[h, f], hid_other[h, f]], 0) for f in picked], 1)
            grad = jnp.concatenate([jnp.concatenate([grad_in[h, f], grad_other[h, f]], 0) for f in picked], 1)
            y_out = dot(w_out, hid)
            y_in = dot(w_in, grad)
            for g, f in enumerate(picked):
                cols = slice(g * width, (g + 1) * width)
                for k in range(3):
                    out_terms.setdefault(f - k + 1, []).append(y_out[k * own_c : (k + 1) * own_c, cols])
                for i in range(3):
                    at = i * 3 * own_c
                    total = (
                        y_in[at + own_c : at + 2 * own_c, cols]
                        + moved(y_in[at : at + own_c, cols], -1)
                        + moved(y_in[at + 2 * own_c : at + 3 * own_c, cols], 1)
                    )
                    if h == 0 or i == 2:
                        ig_acc[f, h + i] = total
                    else:
                        ig_acc[f, h + i] += total
        for f, terms in out_terms.items():
            total = functools.reduce(lambda a, b: a + b, terms)
            if f < 0:
                out_edges[0, h] = total.astype(BF16)
            elif f >= frames:
                out_edges[1, h] = total.astype(BF16)
            else:
                out[f, h] = total

    odd = lax.rem(lax.axis_index("tm"), 2) if fast else 1
    high = jnp.where(lax.axis_index("axial") == 0, rows + 1, 0) if fast else 0
    out_a[...] = out_edges[1 - odd]
    out_b[...] = out_edges[odd]
    for f in range(frames):
        ig_a[f] = ig_acc[f, high].astype(BF16)
        ig_b[f] = ig_acc[f, rows + 1].astype(BF16)
        for h in range(rows):
            ig[f, h] = ig_acc[f, h + 1]


def unpack(packed, acc, sg, tg):
    channels, mid = tg.shape[1:]
    for at, lane, source, column, depth, total in pieces(*acc.shape)[0]:
        acc[source : source + depth, column : column + total] = packed[at : at + depth, lane : lane + total]
    for i in range(3):
        rows = slice(i * channels, (i + 1) * channels)
        for j in range(3):
            sg[i, j] = acc[rows, j * mid : (j + 1) * mid]
        tg[2 - i] = acc[rows, 3 * mid :]


def add_edges(axial_count, own, from_lo, from_hi, ig_own, ig_from_lo, ig_from_hi, out, ig):
    frames, rows = own.shape[:2]
    axial = lax.axis_index("axial")
    has_lo = (axial > 0).astype(F32)
    has_hi = (axial < axial_count - 1).astype(F32)
    for f in range(frames):
        for h in range(rows):
            total = own[f, h]
            if f == 0:
                total = total + from_lo(h).astype(F32)
            if f == frames - 1:
                total = total + from_hi(h).astype(F32)
            out[f, h] = total.astype(BF16)
            total = ig_own[f, h]
            if h == 0:
                total = total + ig_from_lo(f).astype(F32) * has_lo
            if h == rows - 1:
                total = total + ig_from_hi(f).astype(F32) * has_hi
            ig[f, h] = total.astype(BF16)


def last_kernel(own, ig_own, half_0, half_1, across, near, far, ig_edge, out, ig, sg, tg, packed, acc, edges):
    frames, rows, own_c, width = own.shape
    size = half_0.shape[0]
    odd = lax.rem(lax.axis_index("tm"), 2)
    edges[1 - odd] = near[size:].reshape(rows, own_c, width)
    edges[odd] = far[size:].reshape(rows, own_c, width)
    add_edges(
        2,
        own,
        lambda h: edges[0, h],
        lambda h: edges[1, h],
        ig_own,
        lambda f: ig_edge[f],
        lambda f: ig_edge[f],
        out,
        ig,
    )
    packed[:size] = half_0[...].astype(F32) + across[...].astype(F32)
    packed[size:] = half_1[...].astype(F32) + far[:size].astype(F32)
    unpack(packed, acc, sg, tg)


def last_kernel_general(axial_count, *refs):
    own, ig_own, half_0, half_1, from_lo, from_hi, ig_from_lo, ig_from_hi, out, ig, sg, tg, packed, acc, edges = refs
    add_edges(
        axial_count,
        own,
        lambda h: from_lo[h],
        lambda h: from_hi[h],
        ig_own,
        lambda f: ig_from_lo[f],
        lambda f: ig_from_hi[f],
        out,
        ig,
    )
    size = half_0.shape[0]
    packed[:size] = half_0[...]
    packed[size:] = half_1[...]
    unpack(packed, acc, sg, tg)


def call(kernel, name, out_shape, count, limit, scratch=(), in_specs=None, flops=0):
    return pl.pallas_call(
        kernel,
        out_shape=out_shape,
        in_specs=in_specs or [VMEM] * count,
        out_specs=[VMEM] * len(out_shape),
        scratch_shapes=list(scratch),
        compiler_params=pltpu.CompilerParams(vmem_limit_bytes=int(limit * 1024 * 1024)),
        cost_estimate=pl.CostEstimate(flops=flops, bytes_accessed=1 << 20, transcendentals=0) if flops else None,
        name=name,
    )


def shards(frames_in, spatial_weight, temporal_weight, upstream):
    frames, rows, channels, width = frames_in.shape
    mid = temporal_weight.shape[1]
    axial_count = lax.axis_size("axial")
    tm_count = lax.axis_size("tm")
    core_count = lax.axis_size("chan")
    rank_count = tm_count * axial_count
    axial = lax.axis_index("axial")
    own_c = channels // core_count
    group = 2 if frames % 2 == 0 else 1
    dims = (frames, rows, channels, width, mid, own_c, rank_count, axial_count, group)
    size = half_rows(3 * channels, 4 * mid)
    sds = jax.ShapeDtypeStruct

    split = axial_count == 2 and frames % 2 == 0
    edge_count = frames // 2 if split else frames
    turned = jnp.swapaxes(temporal_weight, 1, 2)
    edge, frame = call(
        functools.partial(stage_kernel, split),
        "stage",
        [sds((edge_count, channels, width), BF16), sds((rows, channels, width), BF16)],
        4,
        60,
        [pltpu.SemaphoreType.DMA((2,))],
        [HBM] * 4,
    )(frames_in, upstream, spatial_weight, turned)
    frame = lax.ppermute(frame, ("tm", "chan"), facing(tm_count))
    tw_other = lax.ppermute(turned, "chan", ring(2, 1))
    if split:
        edge = lax.ppermute(edge, "axial", ring(2, 1))
    else:
        edge = lax.ppermute(edge, ("axial", "chan"), facing(axial_count))
    sw_other = lax.ppermute(spatial_weight, "chan", ring(2, 1))

    own_shape = (frames, rows, own_c, width)
    inner = (inner_rows(axial_count, rows)[1], frames - 2, padded(mid), width)
    cells = (rows, frames, padded(mid), width)
    xp_shape = (frames, rows + 2, channels, width)
    up_shape = (frames + 2, rows, channels, width)
    total = (3 * channels, 4 * mid)
    forms = [pltpu.VMEM((3 * mid, 3 * channels), F32), pltpu.VMEM((mid, 3 * channels), F32)]
    fast = axial_count == 2 and tm_count == 4
    hid, grad, acc, xp, up, w_taps, w_act = call(
        functools.partial(inner_kernel, dims),
        "inner_cells",
        [
            sds(inner, BF16),
            sds(inner, BF16),
            sds(total, F32),
            sds(xp_shape, BF16),
            sds(up_shape, BF16),
            sds((3 * mid, 3 * channels), BF16),
            sds((mid, 3 * channels), BF16),
        ],
        4,
        16,
        forms,
        flops=1 << 31,
    )(frames_in, upstream, spatial_weight, turned)
    edge, frame, acc = lax.optimization_barrier((edge, frame, acc))
    swapped = lax.ppermute(jnp.concatenate([edge, frame], 0), "chan", ring(2, 1))
    hid, grad, xp, up, half_0, half_1 = call(
        functools.partial(grads_kernel, dims),
        "weight_grads",
        [
            sds(cells, BF16),
            sds(cells, BF16),
            sds(xp_shape, BF16),
            sds(up_shape, BF16),
            sds((size, LANES), BF16 if fast else F32),
            sds((size, LANES), BF16 if fast else F32),
        ],
        10,
        16,
        [
            pltpu.VMEM((2 * edge_count, channels, width), BF16),
            pltpu.VMEM(total, F32),
            pltpu.VMEM((2 * size, LANES), F32),
        ],
    )(hid, grad, acc, xp, up, edge, frame, swapped, w_taps, w_act)

    if fast:
        got_0 = lax.ppermute(half_0, "tm", pairs(4, 1))
        got_1 = lax.ppermute(half_1, "axial", ring(2, 1))

    hid_other, grad_other = call(
        functools.partial(others_kernel, dims),
        "other_cells",
        [sds(cells, BF16), sds(cells, BF16)],
        4,
        16,
        forms,
        flops=1 << 31,
    )(xp, up, sw_other, tw_other)

    own_shape = (frames, rows, own_c, width)
    out_edge, ig_edge = sds((rows, own_c, width), BF16), sds((frames, own_c, width), BF16)
    out_own, out_a, out_b, ig_own, ig_a, ig_b = call(
        functools.partial(fields_kernel, dims, fast),
        "field_products",
        [sds(own_shape, F32), out_edge, out_edge, sds(own_shape, F32), ig_edge, ig_edge],
        8,
        16,
        [
            pltpu.VMEM((3 * own_c, 2 * padded(mid)), BF16),
            pltpu.VMEM((9 * own_c, 2 * padded(mid)), BF16),
            pltpu.VMEM((frames, rows + 2, own_c, width), F32),
            pltpu.VMEM((2, rows, own_c, width), BF16),
        ],
        flops=1 << 31,
    )(hid, grad, hid_other, grad_other, spatial_weight, turned, sw_other, tw_other)

    outs = [
        sds(own_shape, BF16),
        sds(own_shape, BF16),
        sds((3, 3, channels, mid), F32),
        sds((3, channels, mid), F32),
    ]
    scratch = [
        pltpu.VMEM((2 * size, LANES), F32),
        pltpu.VMEM(total, F32),
        pltpu.VMEM((2, rows, own_c, width), BF16),
    ]
    if fast:
        got_0, out_a, out_b, ig_a = lax.optimization_barrier((got_0, out_a, out_b, ig_a))
        half_0 = lax.optimization_barrier(half_0 + got_0)
        apart = lax.ppermute(half_0, "tm", pairs(4, 2))
        half_1 = lax.optimization_barrier(half_1 + got_1)
        near = lax.ppermute(jnp.concatenate([half_1, out_a.reshape(-1, width)], 0), "tm", pairs(4, 1))
        half_1 = lax.optimization_barrier(half_1 + near[:size])
        far = lax.ppermute(jnp.concatenate([half_1, out_b.reshape(-1, width)], 0), "tm", pairs(4, 3))
        apart, half_1 = lax.optimization_barrier((apart, half_1))
        half_0 = lax.optimization_barrier(half_0 + apart)
        across = lax.ppermute(half_0, "axial", ring(2, 1))
        ig_edge = lax.ppermute(ig_a, "axial", ring(2, 1))
        results = call(last_kernel, "last", outs, 8, 8, scratch)(
            out_own, ig_own, half_0, half_1, across, near, far, ig_edge
        )
    else:
        half_0, half_1 = lax.psum((half_0, half_1), ("tm", "axial"))
        from_hi = lax.ppermute(out_a, "tm", ring(tm_count, -1))
        from_lo = lax.ppermute(out_b, "tm", ring(tm_count, 1))
        ig_from_hi = lax.ppermute(ig_a, "axial", ring(axial_count, -1))
        ig_from_lo = lax.ppermute(ig_b, "axial", ring(axial_count, 1))
        results = call(functools.partial(last_kernel_general, axial_count), "last", outs, 8, 8, scratch)(
            out_own, ig_own, half_0, half_1, from_lo, from_hi, ig_from_lo, ig_from_hi
        )
    output, input_grad, spatial_grad, temporal_grad = results
    return output, input_grad, spatial_grad, jnp.swapaxes(temporal_grad, 1, 2)


def solution(mesh):
    placed = (
        P(("parts", "tm"), "axial", None, None),
        P("parts", None, None, "chan"),
        P("parts", "chan", None),
        P(("parts", "tm"), "axial", None, None),
    )
    return jax.shard_map(
        shards,
        mesh=mesh,
        in_specs=placed,
        out_specs=(
            P(("parts", "tm"), "axial", "chan", None),
            P(("parts", "tm"), "axial", "chan", None),
            P("parts", None, None, "chan"),
            P("parts", "chan", None),
        ),
        check_vma=False,
    )
```

profile of v0, /device:TPU:0, one launch (start us, length us, event | category | flops | bytes accessed | tf_op | source)
XLA Modules:
  0.0 32.6 jit_solution(353524660054885558)
XLA Ops:
  0.6 0.0 copy-start
  0.6 0.0 copy-start.1
  0.7 0.0 copy-start.2
  0.7 0.0 copy-start.3
  0.7 1.6 %stage.1 = (bf16[3,64,128]{2,1,0:T(8,128)(2,1)}, bf16[4,64,128]{2,1,0:T(8,128)(2,1)}) custom-call(bf16[6,4,64,128]{3,2,1,0:T(8,128)(2,1)} %x.1, bf16[6,4,64,128]{3,2,1,0:T(8,128)(2,1)} %u.1, bf16[3,3,64,72]{3,2,1,0:T(8,128)(2,1)} %refs_4_.1, bf16[3,64,72]{2,1,0:T(8,128)(2,1)} %bitcast.4), custom_call_target="tpu_custom_call" | custom-call | tf_op jit(solution)/shard_map/stage/pallas_call | solution.py:416
  2.3 4.6 %collective-permute-start.1 = (bf16[4,64,128]{2,1,0:T(8,128)(2,1)}, bf16[4,64,128]{2,1,0:T(8,128)(2,1)S(1)}, u32[]{:S(2)}, u32[]{:S(2)}) collective-permute-start(bf16[4,64,128]{2,1,0:T(8,128)(2,1)} %get-tuple-element.42), channel_id=1, source_target_pairs={{0,13},{1,4},{4,1},{5,8},{8,5},{9,12},{12,9},{13,0},{2,15},{3,6},{... | collective-permute-start | bytes 196616 | tf_op jit(solution)/shard_map/ppermute | solution.py:425
  6.8 1.5 %collective-permute-start = (bf16[3,64,128]{2,1,0:T(8,128)(2,1)}, bf16[3,64,128]{2,1,0:T(8,128)(2,1)S(1)}, u32[]{:S(2)}, u32[]{:S(2)}) collective-permute-start(bf16[3,64,128]{2,1,0:T(8,128)(2,1)} %get-tuple-element.41), channel_id=1, source_target_pairs={{0,2},{2,0},{1,3},{3,1},{4,6},{6,4},{5,7},{7,5},{8,10},{10,8},{9,1... | collective-permute-start | bytes 147464 | tf_op jit(solution)/shard_map/ppermute | solution.py:428
  8.3 0.0 copy-done
  8.3 0.0 copy-done.1
  8.3 0.0 copy-done.2
  8.3 0.0 copy-done.3
  8.3 1.2 %inner_cells.1 = (bf16[3,4,80,128]{3,2,1,0:T(8,128)(2,1)S(1)}, bf16[3,4,80,128]{3,2,1,0:T(8,128)(2,1)S(1)}, f32[192,288]{1,0:T(8,128)S(1)}, bf16[6,6,64,128]{3,2...) custom-call(bf16[6,4,64,128]{3,2,1,0:T(8,128)(2,1)S(1)} %copy-done, ...), custom_call_target="tpu_custom_call" | custom-call | flops 2147483648 | bytes 1048576 | tf_op jit(solution)/shard_map/inner_cells/pallas_call | solution.py:441
  9.6 1.5 %collective-permute-done.refs_5_ = bf16[3,64,128]{2,1,0:T(8,128)(2,1)S(1)} collective-permute-done((bf16[3,64,128]{2,1,0:T(8,128)(2,1)}, bf16[3,64,128]{2,1,0:T(8,128)(2,1)S(1)}, u32[]{:S(2)}, u32[]{:S(2)}) %collective-permute-start) | collective-permute-done | bytes 49184 | tf_op jit(solution)/shard_map/ppermute | solution.py:428
  11.1 0.0 collective-permute-done.1.refs_6_
  11.1 0.1 collective-permute-start.2
  11.2 0.5 %collective-permute-start.3 = (bf16[3,3,64,72]{3,2,1,0:T(8,128)(2,1)S(1)}, bf16[3,3,64,72]{3,2,1,0:T(8,128)(2,1)S(1)}, u32[]{:S(2)}, u32[]{:S(2)}) collective-permute-start(bf16[3,3,64,72]{3,2,1,0:T(8,128)(2,1)S(1)} %copy-done.2), channel_id=1, source_target_pairs={{0,1},{1,0},{2,3},{3,2},{4,5},{5,4},{6,7},{7,6},{8,9},{9,8},{10,11... | collective-permute-start | bytes 248840 | tf_op jit(solution)/shard_map/ppermute | solution.py:431
  11.7 0.1 collective-permute-start.4
  11.8 0.7 %collective-permute-done.2.refs_7_ = bf16[7,64,128]{2,1,0:T(8,128)(2,1)S(1)} collective-permute-done((bf16[7,64,128]{2,1,0:T(8,128)(2,1)S(1)}, bf16[7,64,128]{2,1,0:T(8,128)(2,1)S(1)}, u32[]{:S(2)}, u32[]{:S(2)}) %collective-permute-start.2) | collective-permute-done | bytes 114720 | tf_op jit(solution)/shard_map/ppermute | solution.py:459
  12.5 1.3 %weight_grads.1 = (bf16[4,6,80,128]{3,2,1,0:T(8,128)(2,1)S(1)}, bf16[4,6,80,128]{3,2,1,0:T(8,128)(2,1)S(1)}, bf16[6,6,64,128]{3,2,1,0:T(8,128)(2,1)S(1)}, bf16[8...) custom-call(bf16[3,4,80,128]{3,2,1,0:T(8,128)(2,1)S(1)} %get-tuple-element.39.refs_0_, ...), custom_call_target="tpu_custom_call" | custom-call | tf_op jit(solution)/shard_map/weight_grads/pallas_call | solution.py:460
  13.8 1.6 %collective-permute-start.7 = (bf16[224,128]{1,0:T(8,128)(2,1)S(1)}, bf16[224,128]{1,0:T(8,128)(2,1)S(1)}, u32[]{:S(2)}, u32[]{:S(2)}) collective-permute-start(bf16[224,128]{1,0:T(8,128)(2,1)S(1)} %get-tuple-element.64), channel_id=1, source_target_pairs={{0,2},{2,0},{1,3},{3,1},{4,6},{6,4},{5,7},{7,5},{8,10},{10,8},{9,1... | collective-permute-start | bytes 172040 | tf_op jit(solution)/shard_map/ppermute | solution.py:482
  15.4 0.0 collective-permute-start.5
  15.4 0.0 collective-permute-done.4.refs_3_.refs_7_
  15.4 0.0 collective-permute-done.3.refs_2_.refs_6_
  15.4 0.9 %other_cells.1 = (bf16[4,6,80,128]{3,2,1,0:T(8,128)(2,1)S(1)}, bf16[4,6,80,128]{3,2,1,0:T(8,128)(2,1)S(1)}) custom-call(bf16[6,6,64,128]{3,2,1,0:T(8,128)(2,1)S(1)} %get-tuple-element.53.refs_0_, bf16[8,4,64,128]{3,2,1,0:T(8,128)(2,1)S(1)} %get-tuple-element.54.refs_1_, bf16[3,3,64,72]{3,2,1,0:T(8,128)(2,1)S(1)} %collective-permute-done.3.refs_2_.refs_6_, ...), custom_call_target="tpu_custom_call" | custom-call | flops 2147483648 | bytes 1048576 | tf_op jit(solution)/shard_map/other_cells/pallas_call | solution.py:484
  16.3 1.6 %field_products.1 = (f32[6,4,32,128]{3,2,1,0:T(8,128)S(1)}, bf16[4,32,128]{2,1,0:T(8,128)(2,1)S(1)}, bf16[4,32,128]{2,1,0:T(8,128)(2,1)S(1)}, f32[6,4,32,128]{3,...) custom-call(bf16[4,6,80,128]{3,2,1,0:T(8,128)(2,1)S(1)} %get-tuple-element.51.refs_0_, ...), custom_call_target="tpu_custom_call" | custom-call | flops 2147483648 | bytes 1048576 | tf_op jit(solution)/shard_map/field_products/pallas_call | solution.py:496
  17.8 0.2 collective-permute-done.7
  18.1 1.5 %collective-permute-done.5 = bf16[224,128]{1,0:T(8,128)(2,1)S(1)} collective-permute-done((bf16[224,128]{1,0:T(8,128)(2,1)S(1)}, bf16[224,128]{1,0:T(8,128)(2,1)S(1)}, u32[]{:S(2)}, u32[]{:S(2)}) %collective-permute-start.5) | collective-permute-done | bytes 57376 | tf_op jit(solution)/shard_map/ppermute | solution.py:481
  19.6 0.4 %collective-permute-start.8 = (bf16[352,128]{1,0:T(8,128)(2,1)S(1)}, bf16[352,128]{1,0:T(8,128)(2,1)S(1)}, u32[]{:S(2)}, u32[]{:S(2)}) collective-permute-start(bf16[352,128]{1,0:T(8,128)(2,1)S(1)} %pad_maximum_fusion.1), channel_id=1, source_target_pairs={{0,4},{4,0},{8,12},{12,8},{1,5},{5,1},{9,13},{13,9},{2,6},{6,2},{1... | collective-permute-start | bytes 270344 | tf_op jit(solution)/shard_map/ppermute | solution.py:527
  20.0 1.7 %collective-permute-start.6 = (bf16[224,128]{1,0:T(8,128)(2,1)S(1)}, bf16[224,128]{1,0:T(8,128)(2,1)S(1)}, u32[]{:S(2)}, u32[]{:S(2)}) collective-permute-start(bf16[224,128]{1,0:T(8,128)(2,1)S(1)} %add.12), channel_id=1, source_target_pairs={{0,8},{4,12},{8,0},{12,4},{1,9},{5,13},{9,1},{13,5},{2,10},{6,14},... | collective-permute-start | bytes 172040 | tf_op jit(solution)/shard_map/ppermute | solution.py:525
  21.7 2.8 %collective-permute-done.8.near = bf16[352,128]{1,0:T(8,128)(2,1)S(1)} collective-permute-done((bf16[352,128]{1,0:T(8,128)(2,1)S(1)}, bf16[352,128]{1,0:T(8,128)(2,1)S(1)}, u32[]{:S(2)}, u32[]{:S(2)}) %collective-permute-start.8) | collective-permute-done | bytes 90144 | tf_op jit(solution)/shard_map/ppermute | solution.py:527
  24.5 2.3 %collective-permute-start.10 = (bf16[352,128]{1,0:T(8,128)(2,1)S(1)}, bf16[352,128]{1,0:T(8,128)(2,1)S(1)}, u32[]{:S(2)}, u32[]{:S(2)}) collective-permute-start(bf16[352,128]{1,0:T(8,128)(2,1)S(1)} %pad_maximum_fusion.2), channel_id=1, source_target_pairs={{0,12},{4,8},{8,4},{12,0},{1,13},{5,9},{9,5},{13,1},{2,14},{6,10},... | collective-permute-start | bytes 270344 | tf_op jit(solution)/shard_map/ppermute | solution.py:529
  26.8 0.0 collective-permute-done.6
  26.8 0.1 collective-permute-start.9
  26.9 2.0 %collective-permute-start.11 = (bf16[6,32,128]{2,1,0:T(8,128)(2,1)S(1)}, bf16[6,32,128]{2,1,0:T(8,128)(2,1)S(1)}, u32[]{:S(2)}, u32[]{:S(2)}) collective-permute-start(bf16[6,32,128]{2,1,0:T(8,128)(2,1)S(1)} %get-tuple-element.69), channel_id=1, source_target_pairs={{0,2},{2,0},{1,3},{3,1},{4,6},{6,4},{5,7},{7,5},{8,10},{10,8},{9,1... | collective-permute-start | bytes 147464 | tf_op jit(solution)/shard_map/ppermute | solution.py:533
  28.9 2.7 %collective-permute-done.11.ig_edge = bf16[6,32,128]{2,1,0:T(8,128)(2,1)S(1)} collective-permute-done((bf16[6,32,128]{2,1,0:T(8,128)(2,1)S(1)}, bf16[6,32,128]{2,1,0:T(8,128)(2,1)S(1)}, u32[]{:S(2)}, u32[]{:S(2)}) %collective-permute-start.11) | collective-permute-done | bytes 49184 | tf_op jit(solution)/shard_map/ppermute | solution.py:533
  31.6 0.0 collective-permute-done.9.across
  31.6 0.0 collective-permute-done.10.far
  31.6 1.1 %last.1 = (bf16[6,4,32,128]{3,2,1,0:T(8,128)(2,1)}, bf16[6,4,32,128]{3,2,1,0:T(8,128)(2,1)}, f32[3,3,64,72]{3,2,1,0:T(8,128)}, f32[3,64,72]{2,1,0:T(8,128)}) custom-call(f32[6,4,32,128]{3,2,1,0:T(8,128)S(1)} %get-tuple-element.57.own, f32[6,4,32,128]{3,2,1,0:T(8,128)S(1)} %get-tuple-element.58.ig_own, bf16[224,128]{1,0:T(8,128)(2,1)S(1)} %add.15.half_0, ...), custom_call_target="tpu_custom_call" | custom-call | tf_op jit(solution)/shard_map/last/pallas_call | solution.py:534
  (7 shorter events, 0.1 us)
Async XLA Ops:
  0.6 7.7 %copy-start = (bf16[6,4,64,128]{3,2,1,0:T(8,128)(2,1)S(1)}, bf16[6,4,64,128]{3,2,1,0:T(8,128)(2,1)}, u32[]{:S(2)}) copy-start(bf16[6,4,64,128]{3,2,1,0:T(8,128)(2,1)} %x.1) | copy-start | bytes 1179652
  0.6 7.7 %copy-start.1 = (bf16[6,4,64,128]{3,2,1,0:T(8,128)(2,1)S(1)}, bf16[6,4,64,128]{3,2,1,0:T(8,128)(2,1)}, u32[]{:S(2)}) copy-start(bf16[6,4,64,128]{3,2,1,0:T(8,128)(2,1)} %u.1) | copy-start | bytes 1179652
  0.7 7.7 %copy-start.2 = (bf16[3,3,64,72]{3,2,1,0:T(8,128)(2,1)S(1)}, bf16[3,3,64,72]{3,2,1,0:T(8,128)(2,1)}, u32[]{:S(2)}) copy-start(bf16[3,3,64,72]{3,2,1,0:T(8,128)(2,1)} %refs_4_.1) | copy-start | bytes 248836
  0.7 7.7 %copy-start.3 = (bf16[3,72,64]{1,2,0:T(8,128)(2,1)S(1)}, bf16[3,72,64]{1,2,0:T(8,128)(2,1)}, u32[]{:S(2)}) copy-start(bf16[3,72,64]{1,2,0:T(8,128)(2,1)} %param.6) | copy-start | bytes 82948
  2.3 8.9 %collective-permute-start.1 = (bf16[4,64,128]{2,1,0:T(8,128)(2,1)}, bf16[4,64,128]{2,1,0:T(8,128)(2,1)S(1)}, u32[]{:S(2)}, u32[]{:S(2)}) collective-permute-start(bf16[4,64,128]{2,1,0:T(8,128)(2,1)} %get-tuple-element.42), channel_id=1, source_target_pairs={{0,13},{1,4},{4,1},{5,8},{8,5},{9,12},{12,9},{13,0},{2,15},{3,6},{... | collective-permute-start | bytes 196616 | tf_op jit(solution)/shard_map/ppermute | solution.py:425
  6.8 4.3 %collective-permute-start = (bf16[3,64,128]{2,1,0:T(8,128)(2,1)}, bf16[3,64,128]{2,1,0:T(8,128)(2,1)S(1)}, u32[]{:S(2)}, u32[]{:S(2)}) collective-permute-start(bf16[3,64,128]{2,1,0:T(8,128)(2,1)} %get-tuple-element.41), channel_id=1, source_target_pairs={{0,2},{2,0},{1,3},{3,1},{4,6},{6,4},{5,7},{7,5},{8,10},{10,8},{9,1... | collective-permute-start | bytes 147464 | tf_op jit(solution)/shard_map/ppermute | solution.py:428
  11.1 1.4 %collective-permute-start.2 = (bf16[7,64,128]{2,1,0:T(8,128)(2,1)S(1)}, bf16[7,64,128]{2,1,0:T(8,128)(2,1)S(1)}, u32[]{:S(2)}, u32[]{:S(2)}) collective-permute-start(bf16[7,64,128]{2,1,0:T(8,128)(2,1)S(1)} %pad_maximum_fusion), channel_id=1, source_target_pairs={{0,1},{1,0},{2,3},{3,2},{4,5},{5,4},{6,7},{7,6},{8,9},{9,8},{10,11... | collective-permute-start | bytes 344072 | tf_op jit(solution)/shard_map/ppermute | solution.py:459
  11.2 4.2 %collective-permute-start.3 = (bf16[3,3,64,72]{3,2,1,0:T(8,128)(2,1)S(1)}, bf16[3,3,64,72]{3,2,1,0:T(8,128)(2,1)S(1)}, u32[]{:S(2)}, u32[]{:S(2)}) collective-permute-start(bf16[3,3,64,72]{3,2,1,0:T(8,128)(2,1)S(1)} %copy-done.2), channel_id=1, source_target_pairs={{0,1},{1,0},{2,3},{3,2},{4,5},{5,4},{6,7},{7,6},{8,9},{9,8},{10,11... | collective-permute-start | bytes 248840 | tf_op jit(solution)/shard_map/ppermute | solution.py:431
  11.7 3.7 %collective-permute-start.4 = (bf16[3,64,72]{2,1,0:T(8,128)(2,1)S(1)}, bf16[3,64,72]{2,1,0:T(8,128)(2,1)S(1)}, u32[]{:S(2)}, u32[]{:S(2)}) collective-permute-start(bf16[3,64,72]{2,1,0:T(8,128)(2,1)S(1)} %bitcast.6), channel_id=1, source_target_pairs={{0,1},{1,0},{2,3},{3,2},{4,5},{5,4},{6,7},{7,6},{8,9},{9,8},{10,11... | collective-permute-start | bytes 82952 | tf_op jit(solution)/shard_map/ppermute | solution.py:426
  13.8 4.2 %collective-permute-start.7 = (bf16[224,128]{1,0:T(8,128)(2,1)S(1)}, bf16[224,128]{1,0:T(8,128)(2,1)S(1)}, u32[]{:S(2)}, u32[]{:S(2)}) collective-permute-start(bf16[224,128]{1,0:T(8,128)(2,1)S(1)} %get-tuple-element.64), channel_id=1, source_target_pairs={{0,2},{2,0},{1,3},{3,1},{4,6},{6,4},{5,7},{7,5},{8,10},{10,8},{9,1... | collective-permute-start | bytes 172040 | tf_op jit(solution)/shard_map/ppermute | solution.py:482
  15.4 4.2 %collective-permute-start.5 = (bf16[224,128]{1,0:T(8,128)(2,1)S(1)}, bf16[224,128]{1,0:T(8,128)(2,1)S(1)}, u32[]{:S(2)}, u32[]{:S(2)}) collective-permute-start(bf16[224,128]{1,0:T(8,128)(2,1)S(1)} %get-tuple-element.59), channel_id=1, source_target_pairs={{0,4},{4,0},{8,12},{12,8},{1,5},{5,1},{9,13},{13,9},{2,6},{6,2},{1... | collective-permute-start | bytes 172040 | tf_op jit(solution)/shard_map/ppermute | solution.py:481
  19.6 4.9 %collective-permute-start.8 = (bf16[352,128]{1,0:T(8,128)(2,1)S(1)}, bf16[352,128]{1,0:T(8,128)(2,1)S(1)}, u32[]{:S(2)}, u32[]{:S(2)}) collective-permute-start(bf16[352,128]{1,0:T(8,128)(2,1)S(1)} %pad_maximum_fusion.1), channel_id=1, source_target_pairs={{0,4},{4,0},{8,12},{12,8},{1,5},{5,1},{9,13},{13,9},{2,6},{6,2},{1... | collective-permute-start | bytes 270344 | tf_op jit(solution)/shard_map/ppermute | solution.py:527
  20.0 6.8 %collective-permute-start.6 = (bf16[224,128]{1,0:T(8,128)(2,1)S(1)}, bf16[224,128]{1,0:T(8,128)(2,1)S(1)}, u32[]{:S(2)}, u32[]{:S(2)}) collective-permute-start(bf16[224,128]{1,0:T(8,128)(2,1)S(1)} %add.12), channel_id=1, source_target_pairs={{0,8},{4,12},{8,0},{12,4},{1,9},{5,13},{9,1},{13,5},{2,10},{6,14},... | collective-permute-start | bytes 172040 | tf_op jit(solution)/shard_map/ppermute | solution.py:525
  24.5 7.1 %collective-permute-start.10 = (bf16[352,128]{1,0:T(8,128)(2,1)S(1)}, bf16[352,128]{1,0:T(8,128)(2,1)S(1)}, u32[]{:S(2)}, u32[]{:S(2)}) collective-permute-start(bf16[352,128]{1,0:T(8,128)(2,1)S(1)} %pad_maximum_fusion.2), channel_id=1, source_target_pairs={{0,12},{4,8},{8,4},{12,0},{1,13},{5,9},{9,5},{13,1},{2,14},{6,10},... | collective-permute-start | bytes 270344 | tf_op jit(solution)/shard_map/ppermute | solution.py:529
  26.8 4.8 %collective-permute-start.9 = (bf16[224,128]{1,0:T(8,128)(2,1)S(1)}, bf16[224,128]{1,0:T(8,128)(2,1)S(1)}, u32[]{:S(2)}, u32[]{:S(2)}) collective-permute-start(bf16[224,128]{1,0:T(8,128)(2,1)S(1)} %add.15.half_0), channel_id=1, source_target_pairs={{0,2},{2,0},{1,3},{3,1},{4,6},{6,4},{5,7},{7,5},{8,10},{10,8},{9,1... | collective-permute-start | bytes 172040 | tf_op jit(solution)/shard_map/ppermute | solution.py:532
  26.9 4.7 %collective-permute-start.11 = (bf16[6,32,128]{2,1,0:T(8,128)(2,1)S(1)}, bf16[6,32,128]{2,1,0:T(8,128)(2,1)S(1)}, u32[]{:S(2)}, u32[]{:S(2)}) collective-permute-start(bf16[6,32,128]{2,1,0:T(8,128)(2,1)S(1)} %get-tuple-element.69), channel_id=1, source_target_pairs={{0,2},{2,0},{1,3},{3,1},{4,6},{6,4},{5,7},{7,5},{8,10},{10,8},{9,1... | collective-permute-start | bytes 147464 | tf_op jit(solution)/shard_map/ppermute | solution.py:533
where the time goes:
time: 32.8 us; the launch traced here: 32.6 us
  starting transfers between devices  14.7 us (45%)
  waiting for transfers between devices  9.44 us (29%)
  Pallas kernels  7.6 us (23%)
  between operations  0.74 us (2%)
    ppermute x1, starting transfers between devices, shards(): frame = lax.ppermute(frame, ('tm', 'chan'), facing(tm_count))  4.55 us
    ppermute x1, waiting for transfers between devices, shards(): lax.ppermute(jnp.concatenate([half_1, out_a.reshape(-1, width)], 0), 'tm'...  2.76 us
    ppermute x1, waiting for transfers between devices, shards(): ig_edge = lax.ppermute(ig_a, 'axial', ring(2, 1))  2.68 us
    ppermute x1, starting transfers between devices, shards(): lax.ppermute(jnp.concatenate([half_1, out_b.reshape(-1, width)], 0), 'tm'...  2.28 us
    ppermute x1, starting transfers between devices, shards(): ig_edge = lax.ppermute(ig_a, 'axial', ring(2, 1))  2.01 us
    ppermute x1, starting transfers between devices, shards(): apart = lax.ppermute(half_0, 'tm', pairs(4, 2))  1.72 us
    pallas_call x1, Pallas kernels, shards(): call(functools.partial(stage_kernel, split), 'stage', [sds((edge_count, c...  1.59 us
    pallas_call x1, Pallas kernels, shards(): call(functools.partial(fields_kernel, dims, fast), 'field_products', [sds...  1.58 us
  transfers between devices with their start and end apart: 12, of which 6 were waited for; matrix products, arithmetic and copies ran while one was open for 0% of the time, Pallas kernels for 15%

commit v1 on v0

--- a/solution.py
+++ b/solution.py
@@ -527,10 +527,10 @@
         near = lax.ppermute(jnp.concatenate([half_1, out_a.reshape(-1, width)], 0), "tm", pairs(4, 1))
         half_1 = lax.optimization_barrier(half_1 + near[:size])
         far = lax.ppermute(jnp.concatenate([half_1, out_b.reshape(-1, width)], 0), "tm", pairs(4, 3))
-        apart, half_1 = lax.optimization_barrier((apart, half_1))
+        ig_edge = lax.ppermute(ig_a, "axial", ring(2, 1))
+        apart, half_1, ig_edge = lax.optimization_barrier((apart, half_1, ig_edge))
         half_0 = lax.optimization_barrier(half_0 + apart)
         across = lax.ppermute(half_0, "axial", ring(2, 1))
-        ig_edge = lax.ppermute(ig_a, "axial", ring(2, 1))
         results = call(last_kernel, "last", outs, 8, 8, scratch)(
             out_own, ig_own, half_0, half_1, across, near, far, ig_edge
         )

time: 32.8 us -> 32.3 us (0.985)
  starting transfers between devices: 14.7 us -> 13.3 us
  waiting for transfers between devices: 9.44 us -> 10.4 us
    ppermute x1, waiting for transfers between devices: 0.01 us -> 4.16 us  [shards(): across = lax.ppermute(half_0, 'axial', ring(2, 1))]
    ppermute x1, waiting for transfers between devices: 2.68 us -> 0.01 us  [shards(): ig_edge = lax.ppermute(ig_a, 'axial', ring(2, 1))]
    ppermute x1, starting transfers between devices: 2.01 us -> 0.53 us  [shards(): ig_edge = lax.ppermute(ig_a, 'axial', ring(2, 1))]
    ppermute x1, waiting for transfers between devices: 2.76 us -> 2.23 us  [shards(): lax.ppermute(jnp.concatenate([half_1, out_a.reshape(-1, width)], 0), 'tm'...]
where the time goes in v1:
time: 32.3 us; the launch traced here: 32.1 us
  starting transfers between devices  13.3 us (41%)
  waiting for transfers between devices  10.4 us (32%)
  Pallas kernels  7.6 us (24%)
  between operations  0.75 us (2%)
    ppermute x1, starting transfers between devices, shards(): frame = lax.ppermute(frame, ('tm', 'chan'), facing(tm_count))  4.55 us
    ppermute x1, waiting for transfers between devices, shards(): across = lax.ppermute(half_0, 'axial', ring(2, 1))  4.16 us
    ppermute x1, starting transfers between devices, shards(): lax.ppermute(jnp.concatenate([half_1, out_b.reshape(-1, width)], 0), 'tm'...  2.28 us
    ppermute x1, waiting for transfers between devices, shards(): lax.ppermute(jnp.concatenate([half_1, out_a.reshape(-1, width)], 0), 'tm'...  2.23 us
    ppermute x1, starting transfers between devices, shards(): apart = lax.ppermute(half_0, 'tm', pairs(4, 2))  1.72 us
    pallas_call x1, Pallas kernels, shards(): call(functools.partial(stage_kernel, split), 'stage', [sds((edge_count, c...  1.59 us
    pallas_call x1, Pallas kernels, shards(): call(functools.partial(fields_kernel, dims, fast), 'field_products', [sds...  1.58 us
    ppermute x1, starting transfers between devices, shards(): got_1 = lax.ppermute(half_1, 'axial', ring(2, 1))  1.57 us
  transfers between devices with their start and end apart: 12, of which 6 were waited for; matrix products, arithmetic and copies ran while one was open for 0% of the time, Pallas kernels for 15%

profile of v1, /device:TPU:0, one launch (start us, length us, event | category | flops | bytes accessed | tf_op | source)
XLA Modules:
  0.0 32.1 jit_solution(17980494260825565314)
XLA Ops:
  0.6 0.0 copy-start
  0.6 0.0 copy-start.1
  0.7 0.0 copy-start.2
  0.7 0.0 copy-start.3
  0.7 1.6 %stage.1 = (bf16[3,64,128]{2,1,0:T(8,128)(2,1)}, bf16[4,64,128]{2,1,0:T(8,128)(2,1)}) custom-call(bf16[6,4,64,128]{3,2,1,0:T(8,128)(2,1)} %x.1, bf16[6,4,64,128]{3,2,1,0:T(8,128)(2,1)} %u.1, bf16[3,3,64,72]{3,2,1,0:T(8,128)(2,1)} %refs_4_.1, bf16[3,64,72]{2,1,0:T(8,128)(2,1)} %bitcast.4), custom_call_target="tpu_custom_call" | custom-call | tf_op jit(solution)/shard_map/stage/pallas_call | solution.py:416
  2.3 4.6 %collective-permute-start.1 = (bf16[4,64,128]{2,1,0:T(8,128)(2,1)}, bf16[4,64,128]{2,1,0:T(8,128)(2,1)S(1)}, u32[]{:S(2)}, u32[]{:S(2)}) collective-permute-start(bf16[4,64,128]{2,1,0:T(8,128)(2,1)} %get-tuple-element.43), channel_id=1, source_target_pairs={{0,13},{1,4},{4,1},{5,8},{8,5},{9,12},{12,9},{13,0},{2,15},{3,6},{... | collective-permute-start | bytes 196616 | tf_op jit(solution)/shard_map/ppermute | solution.py:425
  6.8 1.5 %collective-permute-start = (bf16[3,64,128]{2,1,0:T(8,128)(2,1)}, bf16[3,64,128]{2,1,0:T(8,128)(2,1)S(1)}, u32[]{:S(2)}, u32[]{:S(2)}) collective-permute-start(bf16[3,64,128]{2,1,0:T(8,128)(2,1)} %get-tuple-element.42), channel_id=1, source_target_pairs={{0,2},{2,0},{1,3},{3,1},{4,6},{6,4},{5,7},{7,5},{8,10},{10,8},{9,1... | collective-permute-start | bytes 147464 | tf_op jit(solution)/shard_map/ppermute | solution.py:428
  8.3 0.0 copy-done
  8.3 0.0 copy-done.1
  8.3 0.0 copy-done.2
  8.3 0.0 copy-done.3
  8.3 1.2 %inner_cells.1 = (bf16[3,4,80,128]{3,2,1,0:T(8,128)(2,1)S(1)}, bf16[3,4,80,128]{3,2,1,0:T(8,128)(2,1)S(1)}, f32[192,288]{1,0:T(8,128)S(1)}, bf16[6,6,64,128]{3,2...) custom-call(bf16[6,4,64,128]{3,2,1,0:T(8,128)(2,1)S(1)} %copy-done, ...), custom_call_target="tpu_custom_call" | custom-call | flops 2147483648 | bytes 1048576 | tf_op jit(solution)/shard_map/inner_cells/pallas_call | solution.py:441
  9.6 1.5 %collective-permute-done.refs_5_ = bf16[3,64,128]{2,1,0:T(8,128)(2,1)S(1)} collective-permute-done((bf16[3,64,128]{2,1,0:T(8,128)(2,1)}, bf16[3,64,128]{2,1,0:T(8,128)(2,1)S(1)}, u32[]{:S(2)}, u32[]{:S(2)}) %collective-permute-start) | collective-permute-done | bytes 49184 | tf_op jit(solution)/shard_map/ppermute | solution.py:428
  11.1 0.0 collective-permute-done.1.refs_6_
  11.1 0.1 collective-permute-start.2
  11.2 0.5 %collective-permute-start.3 = (bf16[3,3,64,72]{3,2,1,0:T(8,128)(2,1)S(1)}, bf16[3,3,64,72]{3,2,1,0:T(8,128)(2,1)S(1)}, u32[]{:S(2)}, u32[]{:S(2)}) collective-permute-start(bf16[3,3,64,72]{3,2,1,0:T(8,128)(2,1)S(1)} %copy-done.2), channel_id=1, source_target_pairs={{0,1},{1,0},{2,3},{3,2},{4,5},{5,4},{6,7},{7,6},{8,9},{9,8},{10,11... | collective-permute-start | bytes 248840 | tf_op jit(solution)/shard_map/ppermute | solution.py:431
  11.7 0.1 collective-permute-start.4
  11.8 0.7 %collective-permute-done.2.refs_7_ = bf16[7,64,128]{2,1,0:T(8,128)(2,1)S(1)} collective-permute-done((bf16[7,64,128]{2,1,0:T(8,128)(2,1)S(1)}, bf16[7,64,128]{2,1,0:T(8,128)(2,1)S(1)}, u32[]{:S(2)}, u32[]{:S(2)}) %collective-permute-start.2) | collective-permute-done | bytes 114720 | tf_op jit(solution)/shard_map/ppermute | solution.py:459
  12.5 1.3 %weight_grads.1 = (bf16[4,6,80,128]{3,2,1,0:T(8,128)(2,1)S(1)}, bf16[4,6,80,128]{3,2,1,0:T(8,128)(2,1)S(1)}, bf16[6,6,64,128]{3,2,1,0:T(8,128)(2,1)S(1)}, bf16[8...) custom-call(bf16[3,4,80,128]{3,2,1,0:T(8,128)(2,1)S(1)} %get-tuple-element.40.refs_0_, ...), custom_call_target="tpu_custom_call" | custom-call | tf_op jit(solution)/shard_map/weight_grads/pallas_call | solution.py:460
  13.8 1.6 %collective-permute-start.7 = (bf16[224,128]{1,0:T(8,128)(2,1)S(1)}, bf16[224,128]{1,0:T(8,128)(2,1)S(1)}, u32[]{:S(2)}, u32[]{:S(2)}) collective-permute-start(bf16[224,128]{1,0:T(8,128)(2,1)S(1)} %get-tuple-element.65), channel_id=1, source_target_pairs={{0,2},{2,0},{1,3},{3,1},{4,6},{6,4},{5,7},{7,5},{8,10},{10,8},{9,1... | collective-permute-start | bytes 172040 | tf_op jit(solution)/shard_map/ppermute | solution.py:482
  15.4 0.0 collective-permute-start.5
  15.4 0.0 collective-permute-done.4.refs_3_.refs_7_
  15.4 0.0 collective-permute-done.3.refs_2_.refs_6_
  15.4 0.9 %other_cells.1 = (bf16[4,6,80,128]{3,2,1,0:T(8,128)(2,1)S(1)}, bf16[4,6,80,128]{3,2,1,0:T(8,128)(2,1)S(1)}) custom-call(bf16[6,6,64,128]{3,2,1,0:T(8,128)(2,1)S(1)} %get-tuple-element.54.refs_0_, bf16[8,4,64,128]{3,2,1,0:T(8,128)(2,1)S(1)} %get-tuple-element.55.refs_1_, bf16[3,3,64,72]{3,2,1,0:T(8,128)(2,1)S(1)} %collective-permute-done.3.refs_2_.refs_6_, ...), custom_call_target="tpu_custom_call" | custom-call | flops 2147483648 | bytes 1048576 | tf_op jit(solution)/shard_map/other_cells/pallas_call | solution.py:484
  16.3 1.6 %field_products.1 = (f32[6,4,32,128]{3,2,1,0:T(8,128)S(1)}, bf16[4,32,128]{2,1,0:T(8,128)(2,1)S(1)}, bf16[4,32,128]{2,1,0:T(8,128)(2,1)S(1)}, f32[6,4,32,128]{3,...) custom-call(bf16[4,6,80,128]{3,2,1,0:T(8,128)(2,1)S(1)} %get-tuple-element.52.refs_0_, ...), custom_call_target="tpu_custom_call" | custom-call | flops 2147483648 | bytes 1048576 | tf_op jit(solution)/shard_map/field_products/pallas_call | solution.py:496
  17.8 0.2 collective-permute-done.7
  18.1 1.5 %collective-permute-done.5 = bf16[224,128]{1,0:T(8,128)(2,1)S(1)} collective-permute-done((bf16[224,128]{1,0:T(8,128)(2,1)S(1)}, bf16[224,128]{1,0:T(8,128)(2,1)S(1)}, u32[]{:S(2)}, u32[]{:S(2)}) %collective-permute-start.5) | collective-permute-done | bytes 57376 | tf_op jit(solution)/shard_map/ppermute | solution.py:481
  19.6 0.4 %collective-permute-start.8 = (bf16[352,128]{1,0:T(8,128)(2,1)S(1)}, bf16[352,128]{1,0:T(8,128)(2,1)S(1)}, u32[]{:S(2)}, u32[]{:S(2)}) collective-permute-start(bf16[352,128]{1,0:T(8,128)(2,1)S(1)} %pad_maximum_fusion.1), channel_id=1, source_target_pairs={{0,4},{4,0},{8,12},{12,8},{1,5},{5,1},{9,13},{13,9},{2,6},{6,2},{1... | collective-permute-start | bytes 270344 | tf_op jit(solution)/shard_map/ppermute | solution.py:527
  20.0 1.7 %collective-permute-start.6 = (bf16[224,128]{1,0:T(8,128)(2,1)S(1)}, bf16[224,128]{1,0:T(8,128)(2,1)S(1)}, u32[]{:S(2)}, u32[]{:S(2)}) collective-permute-start(bf16[224,128]{1,0:T(8,128)(2,1)S(1)} %add.12), channel_id=1, source_target_pairs={{0,8},{4,12},{8,0},{12,4},{1,9},{5,13},{9,1},{13,5},{2,10},{6,14},... | collective-permute-start | bytes 172040 | tf_op jit(solution)/shard_map/ppermute | solution.py:525
  21.7 0.5 %collective-permute-start.9 = (bf16[6,32,128]{2,1,0:T(8,128)(2,1)S(1)}, bf16[6,32,128]{2,1,0:T(8,128)(2,1)S(1)}, u32[]{:S(2)}, u32[]{:S(2)}) collective-permute-start(bf16[6,32,128]{2,1,0:T(8,128)(2,1)S(1)} %get-tuple-element.67), channel_id=1, source_target_pairs={{0,2},{2,0},{1,3},{3,1},{4,6},{6,4},{5,7},{7,5},{8,10},{10,8},{9,1... | collective-permute-start | bytes 147464 | tf_op jit(solution)/shard_map/ppermute | solution.py:530
  22.3 2.2 %collective-permute-done.8.near = bf16[352,128]{1,0:T(8,128)(2,1)S(1)} collective-permute-done((bf16[352,128]{1,0:T(8,128)(2,1)S(1)}, bf16[352,128]{1,0:T(8,128)(2,1)S(1)}, u32[]{:S(2)}, u32[]{:S(2)}) %collective-permute-start.8) | collective-permute-done | bytes 90144 | tf_op jit(solution)/shard_map/ppermute | solution.py:527
  24.5 2.3 %collective-permute-start.11 = (bf16[352,128]{1,0:T(8,128)(2,1)S(1)}, bf16[352,128]{1,0:T(8,128)(2,1)S(1)}, u32[]{:S(2)}, u32[]{:S(2)}) collective-permute-start(bf16[352,128]{1,0:T(8,128)(2,1)S(1)} %pad_maximum_fusion.2), channel_id=1, source_target_pairs={{0,12},{4,8},{8,4},{12,0},{1,13},{5,9},{9,5},{13,1},{2,14},{6,10},... | collective-permute-start | bytes 270344 | tf_op jit(solution)/shard_map/ppermute | solution.py:529
  26.8 0.0 collective-permute-done.9.ig_edge
  26.8 0.0 collective-permute-done.6
  26.8 0.1 collective-permute-start.10
  26.9 4.2 %collective-permute-done.10.across = bf16[224,128]{1,0:T(8,128)(2,1)S(1)} collective-permute-done((bf16[224,128]{1,0:T(8,128)(2,1)S(1)}, bf16[224,128]{1,0:T(8,128)(2,1)S(1)}, u32[]{:S(2)}, u32[]{:S(2)}) %collective-permute-start.10) | collective-permute-done | bytes 57376 | tf_op jit(solution)/shard_map/ppermute | solution.py:533
  31.1 0.0 collective-permute-done.11.far
  31.1 1.1 %last.1 = (bf16[6,4,32,128]{3,2,1,0:T(8,128)(2,1)}, bf16[6,4,32,128]{3,2,1,0:T(8,128)(2,1)}, f32[3,3,64,72]{3,2,1,0:T(8,128)}, f32[3,64,72]{2,1,0:T(8,128)}) custom-call(f32[6,4,32,128]{3,2,1,0:T(8,128)S(1)} %get-tuple-element.58.own, f32[6,4,32,128]{3,2,1,0:T(8,128)S(1)} %get-tuple-element.59.ig_own, bf16[224,128]{1,0:T(8,128)(2,1)S(1)} %add.15.half_0, ...), custom_call_target="tpu_custom_call" | custom-call | tf_op jit(solution)/shard_map/last/pallas_call | solution.py:534
  (7 shorter events, 0.1 us)
Async XLA Ops:
  0.6 7.7 %copy-start = (bf16[6,4,64,128]{3,2,1,0:T(8,128)(2,1)S(1)}, bf16[6,4,64,128]{3,2,1,0:T(8,128)(2,1)}, u32[]{:S(2)}) copy-start(bf16[6,4,64,128]{3,2,1,0:T(8,128)(2,1)} %x.1) | copy-start | bytes 1179652
  0.6 7.7 %copy-start.1 = (bf16[6,4,64,128]{3,2,1,0:T(8,128)(2,1)S(1)}, bf16[6,4,64,128]{3,2,1,0:T(8,128)(2,1)}, u32[]{:S(2)}) copy-start(bf16[6,4,64,128]{3,2,1,0:T(8,128)(2,1)} %u.1) | copy-start | bytes 1179652
  0.7 7.7 %copy-start.2 = (bf16[3,3,64,72]{3,2,1,0:T(8,128)(2,1)S(1)}, bf16[3,3,64,72]{3,2,1,0:T(8,128)(2,1)}, u32[]{:S(2)}) copy-start(bf16[3,3,64,72]{3,2,1,0:T(8,128)(2,1)} %refs_4_.1) | copy-start | bytes 248836
  0.7 7.7 %copy-start.3 = (bf16[3,72,64]{1,2,0:T(8,128)(2,1)S(1)}, bf16[3,72,64]{1,2,0:T(8,128)(2,1)}, u32[]{:S(2)}) copy-start(bf16[3,72,64]{1,2,0:T(8,128)(2,1)} %param.6) | copy-start | bytes 82948
  2.3 8.9 %collective-permute-start.1 = (bf16[4,64,128]{2,1,0:T(8,128)(2,1)}, bf16[4,64,128]{2,1,0:T(8,128)(2,1)S(1)}, u32[]{:S(2)}, u32[]{:S(2)}) collective-permute-start(bf16[4,64,128]{2,1,0:T(8,128)(2,1)} %get-tuple-element.43), channel_id=1, source_target_pairs={{0,13},{1,4},{4,1},{5,8},{8,5},{9,12},{12,9},{13,0},{2,15},{3,6},{... | collective-permute-start | bytes 196616 | tf_op jit(solution)/shard_map/ppermute | solution.py:425
  6.8 4.3 %collective-permute-start = (bf16[3,64,128]{2,1,0:T(8,128)(2,1)}, bf16[3,64,128]{2,1,0:T(8,128)(2,1)S(1)}, u32[]{:S(2)}, u32[]{:S(2)}) collective-permute-start(bf16[3,64,128]{2,1,0:T(8,128)(2,1)} %get-tuple-element.42), channel_id=1, source_target_pairs={{0,2},{2,0},{1,3},{3,1},{4,6},{6,4},{5,7},{7,5},{8,10},{10,8},{9,1... | collective-permute-start | bytes 147464 | tf_op jit(solution)/shard_map/ppermute | solution.py:428
  11.1 1.4 %collective-permute-start.2 = (bf16[7,64,128]{2,1,0:T(8,128)(2,1)S(1)}, bf16[7,64,128]{2,1,0:T(8,128)(2,1)S(1)}, u32[]{:S(2)}, u32[]{:S(2)}) collective-permute-start(bf16[7,64,128]{2,1,0:T(8,128)(2,1)S(1)} %pad_maximum_fusion), channel_id=1, source_target_pairs={{0,1},{1,0},{2,3},{3,2},{4,5},{5,4},{6,7},{7,6},{8,9},{9,8},{10,11... | collective-permute-start | bytes 344072 | tf_op jit(solution)/shard_map/ppermute | solution.py:459
  11.2 4.2 %collective-permute-start.3 = (bf16[3,3,64,72]{3,2,1,0:T(8,128)(2,1)S(1)}, bf16[3,3,64,72]{3,2,1,0:T(8,128)(2,1)S(1)}, u32[]{:S(2)}, u32[]{:S(2)}) collective-permute-start(bf16[3,3,64,72]{3,2,1,0:T(8,128)(2,1)S(1)} %copy-done.2), channel_id=1, source_target_pairs={{0,1},{1,0},{2,3},{3,2},{4,5},{5,4},{6,7},{7,6},{8,9},{9,8},{10,11... | collective-permute-start | bytes 248840 | tf_op jit(solution)/shard_map/ppermute | solution.py:431
  11.7 3.7 %collective-permute-start.4 = (bf16[3,64,72]{2,1,0:T(8,128)(2,1)S(1)}, bf16[3,64,72]{2,1,0:T(8,128)(2,1)S(1)}, u32[]{:S(2)}, u32[]{:S(2)}) collective-permute-start(bf16[3,64,72]{2,1,0:T(8,128)(2,1)S(1)} %bitcast.6), channel_id=1, source_target_pairs={{0,1},{1,0},{2,3},{3,2},{4,5},{5,4},{6,7},{7,6},{8,9},{9,8},{10,11... | collective-permute-start | bytes 82952 | tf_op jit(solution)/shard_map/ppermute | solution.py:426
  13.8 4.2 %collective-permute-start.7 = (bf16[224,128]{1,0:T(8,128)(2,1)S(1)}, bf16[224,128]{1,0:T(8,128)(2,1)S(1)}, u32[]{:S(2)}, u32[]{:S(2)}) collective-permute-start(bf16[224,128]{1,0:T(8,128)(2,1)S(1)} %get-tuple-element.65), channel_id=1, source_target_pairs={{0,2},{2,0},{1,3},{3,1},{4,6},{6,4},{5,7},{7,5},{8,10},{10,8},{9,1... | collective-permute-start | bytes 172040 | tf_op jit(solution)/shard_map/ppermute | solution.py:482
  15.4 4.2 %collective-permute-start.5 = (bf16[224,128]{1,0:T(8,128)(2,1)S(1)}, bf16[224,128]{1,0:T(8,128)(2,1)S(1)}, u32[]{:S(2)}, u32[]{:S(2)}) collective-permute-start(bf16[224,128]{1,0:T(8,128)(2,1)S(1)} %get-tuple-element.60), channel_id=1, source_target_pairs={{0,4},{4,0},{8,12},{12,8},{1,5},{5,1},{9,13},{13,9},{2,6},{6,2},{1... | collective-permute-start | bytes 172040 | tf_op jit(solution)/shard_map/ppermute | solution.py:481
  19.6 4.9 %collective-permute-start.8 = (bf16[352,128]{1,0:T(8,128)(2,1)S(1)}, bf16[352,128]{1,0:T(8,128)(2,1)S(1)}, u32[]{:S(2)}, u32[]{:S(2)}) collective-permute-start(bf16[352,128]{1,0:T(8,128)(2,1)S(1)} %pad_maximum_fusion.1), channel_id=1, source_target_pairs={{0,4},{4,0},{8,12},{12,8},{1,5},{5,1},{9,13},{13,9},{2,6},{6,2},{1... | collective-permute-start | bytes 270344 | tf_op jit(solution)/shard_map/ppermute | solution.py:527
  20.0 6.8 %collective-permute-start.6 = (bf16[224,128]{1,0:T(8,128)(2,1)S(1)}, bf16[224,128]{1,0:T(8,128)(2,1)S(1)}, u32[]{:S(2)}, u32[]{:S(2)}) collective-permute-start(bf16[224,128]{1,0:T(8,128)(2,1)S(1)} %add.12), channel_id=1, source_target_pairs={{0,8},{4,12},{8,0},{12,4},{1,9},{5,13},{9,1},{13,5},{2,10},{6,14},... | collective-permute-start | bytes 172040 | tf_op jit(solution)/shard_map/ppermute | solution.py:525
  21.7 5.1 %collective-permute-start.9 = (bf16[6,32,128]{2,1,0:T(8,128)(2,1)S(1)}, bf16[6,32,128]{2,1,0:T(8,128)(2,1)S(1)}, u32[]{:S(2)}, u32[]{:S(2)}) collective-permute-start(bf16[6,32,128]{2,1,0:T(8,128)(2,1)S(1)} %get-tuple-element.67), channel_id=1, source_target_pairs={{0,2},{2,0},{1,3},{3,1},{4,6},{6,4},{5,7},{7,5},{8,10},{10,8},{9,1... | collective-permute-start | bytes 147464 | tf_op jit(solution)/shard_map/ppermute | solution.py:530
  24.5 6.6 %collective-permute-start.11 = (bf16[352,128]{1,0:T(8,128)(2,1)S(1)}, bf16[352,128]{1,0:T(8,128)(2,1)S(1)}, u32[]{:S(2)}, u32[]{:S(2)}) collective-permute-start(bf16[352,128]{1,0:T(8,128)(2,1)S(1)} %pad_maximum_fusion.2), channel_id=1, source_target_pairs={{0,12},{4,8},{8,4},{12,0},{1,13},{5,9},{9,5},{13,1},{2,14},{6,10},... | collective-permute-start | bytes 270344 | tf_op jit(solution)/shard_map/ppermute | solution.py:529
  26.8 4.2 %collective-permute-start.10 = (bf16[224,128]{1,0:T(8,128)(2,1)S(1)}, bf16[224,128]{1,0:T(8,128)(2,1)S(1)}, u32[]{:S(2)}, u32[]{:S(2)}) collective-permute-start(bf16[224,128]{1,0:T(8,128)(2,1)S(1)} %add.15.half_0), channel_id=1, source_target_pairs={{0,2},{2,0},{1,3},{3,1},{4,6},{6,4},{5,7},{7,5},{8,10},{10,8},{9,1... | collective-permute-start | bytes 172040 | tf_op jit(solution)/shard_map/ppermute | solution.py:533

commit v2 on v1

--- a/solution.py
+++ b/solution.py
@@ -308,6 +308,13 @@
         ig_b[f] = ig_acc[f, rows + 1].astype(BF16)
         for h in range(rows):
             ig[f, h] = ig_acc[f, h + 1]
+
+
+def rest_kernel(dims, fast, *refs):
+    hid, grad, xp, up, sw, tw, sw_other, tw_other = refs[:8]
+    outs, (wf, twf, hid_other, grad_other), scratch = refs[8:14], refs[14:18], refs[18:]
+    others_kernel(dims, xp, up, sw_other, tw_other, hid_other, grad_other, wf, twf)
+    fields_kernel(dims, fast, hid, grad, hid_other, grad_other, sw, tw, sw_other, tw_other, *outs, *scratch)
 
 
 def unpack(packed, acc, sg, tg):
@@ -481,32 +488,25 @@
         got_0 = lax.ppermute(half_0, "tm", pairs(4, 1))
         got_1 = lax.ppermute(half_1, "axial", ring(2, 1))
 
-    hid_other, grad_other = call(
-        functools.partial(others_kernel, dims),
-        "other_cells",
-        [sds(cells, BF16), sds(cells, BF16)],
-        4,
-        16,
-        forms,
-        flops=1 << 31,
-    )(xp, up, sw_other, tw_other)
-
     own_shape = (frames, rows, own_c, width)
     out_edge, ig_edge = sds((rows, own_c, width), BF16), sds((frames, own_c, width), BF16)
     out_own, out_a, out_b, ig_own, ig_a, ig_b = call(
-        functools.partial(fields_kernel, dims, fast),
+        functools.partial(rest_kernel, dims, fast),
         "field_products",
         [sds(own_shape, F32), out_edge, out_edge, sds(own_shape, F32), ig_edge, ig_edge],
         8,
         16,
-        [
+        forms
+        + [
+            pltpu.VMEM(cells, BF16),
+            pltpu.VMEM(cells, BF16),
             pltpu.VMEM((3 * own_c, 2 * padded(mid)), BF16),
             pltpu.VMEM((9 * own_c, 2 * padded(mid)), BF16),
             pltpu.VMEM((frames, rows + 2, own_c, width), F32),
             pltpu.VMEM((2, rows, own_c, width), BF16),
         ],
         flops=1 << 31,
-    )(hid, grad, hid_other, grad_other, spatial_weight, turned, sw_other, tw_other)
+    )(hid, grad, xp, up, spatial_weight, turned, sw_other, tw_other)
 
     outs = [
         sds(own_shape, BF16),

time: 32.3 us -> 31.8 us (0.985)
  Pallas kernels: 7.6 us -> 7.27 us
    ppermute x1, starting transfers between devices: 2.28 us -> 1.7 us  [shards(): lax.ppermute(jnp.concatenate([half_1, out_b.reshape(-1, width)], 0), 'tm'...]
    ppermute x1, starting transfers between devices: 0.07 us -> 0.62 us  [shards(): across = lax.ppermute(half_0, 'axial', ring(2, 1))]
    ppermute x1, waiting for transfers between devices: 4.16 us -> 3.63 us  [shards(): across = lax.ppermute(half_0, 'axial', ring(2, 1))]
    ppermute x1, waiting for transfers between devices: 0.01 us -> 0.41 us  [shards(): lax.ppermute(jnp.concatenate([half_1, out_b.reshape(-1, width)], 0), 'tm'...]
    ppermute x1, waiting for transfers between devices: 0.22 us -> 0.57 us  [shards(): got_1 = lax.ppermute(half_1, 'axial', ring(2, 1))]
    ppermute x1, starting transfers between devices: 0.4 us -> 0.07 us  [shards(): lax.ppermute(jnp.concatenate([half_1, out_a.reshape(-1, width)], 0), 'tm'...]
    pallas_call x2 -> x1, Pallas kernels: 2.43 us -> 2.1 us  [shards(): call(functools.partial(rest_kernel, dims, fast), 'field_products', [sds(o...]
    ppermute x1, waiting for transfers between devices: 2.23 us -> 1.9 us  [shards(): lax.ppermute(jnp.concatenate([half_1, out_a.reshape(-1, width)], 0), 'tm'...]
  transfers between devices with their start and end apart: 12 -> 12, of which waited for: 6 -> 7; matrix products, arithmetic and copies ran while one was open for 0% -> 0% of each run, Pallas kernels for 15% -> 15%
where the time goes in v2:
time: 31.8 us; the launch traced here: 31.6 us
  starting transfers between devices  13.2 us (42%)
  waiting for transfers between devices  10.3 us (32%)
  Pallas kernels  7.27 us (23%)
  between operations  0.74 us (2%)
    ppermute x1, starting transfers between devices, shards(): frame = lax.ppermute(frame, ('tm', 'chan'), facing(tm_count))  4.55 us
    ppermute x1, waiting for transfers between devices, shards(): across = lax.ppermute(half_0, 'axial', ring(2, 1))  3.63 us
    pallas_call x1, Pallas kernels, shards(): call(functools.partial(rest_kernel, dims, fast), 'field_products', [sds(o...  2.1 us
    ppermute x1, starting transfers between devices, shards(): apart = lax.ppermute(half_0, 'tm', pairs(4, 2))  2.05 us
    ppermute x1, waiting for transfers between devices, shards(): lax.ppermute(jnp.concatenate([half_1, out_a.reshape(-1, width)], 0), 'tm'...  1.9 us
    ppermute x1, starting transfers between devices, shards(): lax.ppermute(jnp.concatenate([half_1, out_b.reshape(-1, width)], 0), 'tm'...  1.7 us
    pallas_call x1, Pallas kernels, shards(): call(functools.partial(stage_kernel, split), 'stage', [sds((edge_count, c...  1.59 us
    ppermute x1, starting transfers between devices, shards(): got_1 = lax.ppermute(half_1, 'axial', ring(2, 1))  1.56 us
  transfers between devices with their start and end apart: 12, of which 7 were waited for; matrix products, arithmetic and copies ran while one was open for 0% of the time, Pallas kernels for 15%

profile of v2, /device:TPU:0, one launch (start us, length us, event | category | flops | bytes accessed | tf_op | source)
XLA Modules:
  0.0 31.6 jit_solution(10846376666035017799)
XLA Ops:
  0.6 0.0 copy-start
  0.6 0.0 copy-start.1
  0.7 0.0 copy-start.2
  0.7 0.0 copy-start.3
  0.7 1.6 %stage.1 = (bf16[3,64,128]{2,1,0:T(8,128)(2,1)}, bf16[4,64,128]{2,1,0:T(8,128)(2,1)}) custom-call(bf16[6,4,64,128]{3,2,1,0:T(8,128)(2,1)} %x.1, bf16[6,4,64,128]{3,2,1,0:T(8,128)(2,1)} %u.1, bf16[3,3,64,72]{3,2,1,0:T(8,128)(2,1)} %refs_4_.1, bf16[3,64,72]{2,1,0:T(8,128)(2,1)} %bitcast.4), custom_call_target="tpu_custom_call" | custom-call | tf_op jit(solution)/shard_map/stage/pallas_call | solution.py:423
  2.3 4.6 %collective-permute-start.1 = (bf16[4,64,128]{2,1,0:T(8,128)(2,1)}, bf16[4,64,128]{2,1,0:T(8,128)(2,1)S(1)}, u32[]{:S(2)}, u32[]{:S(2)}) collective-permute-start(bf16[4,64,128]{2,1,0:T(8,128)(2,1)} %get-tuple-element.41), channel_id=1, source_target_pairs={{0,13},{1,4},{4,1},{5,8},{8,5},{9,12},{12,9},{13,0},{2,15},{3,6},{... | collective-permute-start | bytes 196616 | tf_op jit(solution)/shard_map/ppermute | solution.py:432
  6.8 1.5 %collective-permute-start = (bf16[3,64,128]{2,1,0:T(8,128)(2,1)}, bf16[3,64,128]{2,1,0:T(8,128)(2,1)S(1)}, u32[]{:S(2)}, u32[]{:S(2)}) collective-permute-start(bf16[3,64,128]{2,1,0:T(8,128)(2,1)} %get-tuple-element.40), channel_id=1, source_target_pairs={{0,2},{2,0},{1,3},{3,1},{4,6},{6,4},{5,7},{7,5},{8,10},{10,8},{9,1... | collective-permute-start | bytes 147464 | tf_op jit(solution)/shard_map/ppermute | solution.py:435
  8.3 0.0 copy-done
  8.3 0.0 copy-done.1
  8.3 0.0 copy-done.2
  8.3 0.0 copy-done.3
  8.3 1.2 %inner_cells.1 = (bf16[3,4,80,128]{3,2,1,0:T(8,128)(2,1)S(1)}, bf16[3,4,80,128]{3,2,1,0:T(8,128)(2,1)S(1)}, f32[192,288]{1,0:T(8,128)S(1)}, bf16[6,6,64,128]{3,2...) custom-call(bf16[6,4,64,128]{3,2,1,0:T(8,128)(2,1)S(1)} %copy-done, ...), custom_call_target="tpu_custom_call" | custom-call | flops 2147483648 | bytes 1048576 | tf_op jit(solution)/shard_map/inner_cells/pallas_call | solution.py:448
  9.6 1.5 %collective-permute-done.refs_5_ = bf16[3,64,128]{2,1,0:T(8,128)(2,1)S(1)} collective-permute-done((bf16[3,64,128]{2,1,0:T(8,128)(2,1)}, bf16[3,64,128]{2,1,0:T(8,128)(2,1)S(1)}, u32[]{:S(2)}, u32[]{:S(2)}) %collective-permute-start) | collective-permute-done | bytes 49184 | tf_op jit(solution)/shard_map/ppermute | solution.py:435
  11.1 0.0 collective-permute-done.1.refs_6_
  11.1 0.1 collective-permute-start.2
  11.2 0.5 %collective-permute-start.3 = (bf16[3,3,64,72]{3,2,1,0:T(8,128)(2,1)S(1)}, bf16[3,3,64,72]{3,2,1,0:T(8,128)(2,1)S(1)}, u32[]{:S(2)}, u32[]{:S(2)}) collective-permute-start(bf16[3,3,64,72]{3,2,1,0:T(8,128)(2,1)S(1)} %copy-done.2), channel_id=1, source_target_pairs={{0,1},{1,0},{2,3},{3,2},{4,5},{5,4},{6,7},{7,6},{8,9},{9,8},{10,11... | collective-permute-start | bytes 248840 | tf_op jit(solution)/shard_map/ppermute | solution.py:438
  11.7 0.1 collective-permute-start.4
  11.8 0.7 %collective-permute-done.2.refs_7_ = bf16[7,64,128]{2,1,0:T(8,128)(2,1)S(1)} collective-permute-done((bf16[7,64,128]{2,1,0:T(8,128)(2,1)S(1)}, bf16[7,64,128]{2,1,0:T(8,128)(2,1)S(1)}, u32[]{:S(2)}, u32[]{:S(2)}) %collective-permute-start.2) | collective-permute-done | bytes 114720 | tf_op jit(solution)/shard_map/ppermute | solution.py:466
  12.5 1.3 %weight_grads.1 = (bf16[4,6,80,128]{3,2,1,0:T(8,128)(2,1)S(1)}, bf16[4,6,80,128]{3,2,1,0:T(8,128)(2,1)S(1)}, bf16[6,6,64,128]{3,2,1,0:T(8,128)(2,1)S(1)}, bf16[8...) custom-call(bf16[3,4,80,128]{3,2,1,0:T(8,128)(2,1)S(1)} %get-tuple-element.38.refs_0_, ...), custom_call_target="tpu_custom_call" | custom-call | tf_op jit(solution)/shard_map/weight_grads/pallas_call | solution.py:467
  13.8 1.6 %collective-permute-start.7 = (bf16[224,128]{1,0:T(8,128)(2,1)S(1)}, bf16[224,128]{1,0:T(8,128)(2,1)S(1)}, u32[]{:S(2)}, u32[]{:S(2)}) collective-permute-start(bf16[224,128]{1,0:T(8,128)(2,1)S(1)} %get-tuple-element.61), channel_id=1, source_target_pairs={{0,2},{2,0},{1,3},{3,1},{4,6},{6,4},{5,7},{7,5},{8,10},{10,8},{9,1... | collective-permute-start | bytes 172040 | tf_op jit(solution)/shard_map/ppermute | solution.py:489
  15.4 0.0 collective-permute-start.5
  15.4 0.0 collective-permute-done.4.refs_7_
  15.4 0.0 collective-permute-done.3.refs_6_
  15.4 2.1 %field_products.1 = (f32[6,4,32,128]{3,2,1,0:T(8,128)S(1)}, bf16[4,32,128]{2,1,0:T(8,128)(2,1)S(1)}, bf16[4,32,128]{2,1,0:T(8,128)(2,1)S(1)}, f32[6,4,32,128]{3,...) custom-call(bf16[4,6,80,128]{3,2,1,0:T(8,128)(2,1)S(1)} %get-tuple-element.50.refs_0_, ...), custom_call_target="tpu_custom_call" | custom-call | flops 2147483648 | bytes 1048576 | tf_op jit(solution)/shard_map/field_products/pallas_call | solution.py:493
  17.5 0.6 %collective-permute-done.7 = bf16[224,128]{1,0:T(8,128)(2,1)S(1)} collective-permute-done((bf16[224,128]{1,0:T(8,128)(2,1)S(1)}, bf16[224,128]{1,0:T(8,128)(2,1)S(1)}, u32[]{:S(2)}, u32[]{:S(2)}) %collective-permute-start.7) | collective-permute-done | bytes 57376 | tf_op jit(solution)/shard_map/ppermute | solution.py:489
  18.1 1.5 %collective-permute-done.5 = bf16[224,128]{1,0:T(8,128)(2,1)S(1)} collective-permute-done((bf16[224,128]{1,0:T(8,128)(2,1)S(1)}, bf16[224,128]{1,0:T(8,128)(2,1)S(1)}, u32[]{:S(2)}, u32[]{:S(2)}) %collective-permute-start.5) | collective-permute-done | bytes 57376 | tf_op jit(solution)/shard_map/ppermute | solution.py:488
  19.6 0.1 collective-permute-start.8
  19.7 2.0 %collective-permute-start.6 = (bf16[224,128]{1,0:T(8,128)(2,1)S(1)}, bf16[224,128]{1,0:T(8,128)(2,1)S(1)}, u32[]{:S(2)}, u32[]{:S(2)}) collective-permute-start(bf16[224,128]{1,0:T(8,128)(2,1)S(1)} %add.12), channel_id=1, source_target_pairs={{0,8},{4,12},{8,0},{12,4},{1,9},{5,13},{9,1},{13,5},{2,10},{6,14},... | collective-permute-start | bytes 172040 | tf_op jit(solution)/shard_map/ppermute | solution.py:525
  21.7 0.5 %collective-permute-start.9 = (bf16[6,32,128]{2,1,0:T(8,128)(2,1)S(1)}, bf16[6,32,128]{2,1,0:T(8,128)(2,1)S(1)}, u32[]{:S(2)}, u32[]{:S(2)}) collective-permute-start(bf16[6,32,128]{2,1,0:T(8,128)(2,1)S(1)} %get-tuple-element.63), channel_id=1, source_target_pairs={{0,2},{2,0},{1,3},{3,1},{4,6},{6,4},{5,7},{7,5},{8,10},{10,8},{9,1... | collective-permute-start | bytes 147464 | tf_op jit(solution)/shard_map/ppermute | solution.py:530
  22.3 1.9 %collective-permute-done.8.near = bf16[352,128]{1,0:T(8,128)(2,1)S(1)} collective-permute-done((bf16[352,128]{1,0:T(8,128)(2,1)S(1)}, bf16[352,128]{1,0:T(8,128)(2,1)S(1)}, u32[]{:S(2)}, u32[]{:S(2)}) %collective-permute-start.8) | collective-permute-done | bytes 90144 | tf_op jit(solution)/shard_map/ppermute | solution.py:527
  24.2 1.7 %collective-permute-start.11 = (bf16[352,128]{1,0:T(8,128)(2,1)S(1)}, bf16[352,128]{1,0:T(8,128)(2,1)S(1)}, u32[]{:S(2)}, u32[]{:S(2)}) collective-permute-start(bf16[352,128]{1,0:T(8,128)(2,1)S(1)} %pad_maximum_fusion.2), channel_id=1, source_target_pairs={{0,12},{4,8},{8,4},{12,0},{1,13},{5,9},{9,5},{13,1},{2,14},{6,10},... | collective-permute-start | bytes 270344 | tf_op jit(solution)/shard_map/ppermute | solution.py:529
  25.9 0.0 collective-permute-done.9.ig_edge
  25.9 0.0 collective-permute-done.6
  25.9 0.6 %collective-permute-start.10 = (bf16[224,128]{1,0:T(8,128)(2,1)S(1)}, bf16[224,128]{1,0:T(8,128)(2,1)S(1)}, u32[]{:S(2)}, u32[]{:S(2)}) collective-permute-start(bf16[224,128]{1,0:T(8,128)(2,1)S(1)} %add.15.half_0), channel_id=1, source_target_pairs={{0,2},{2,0},{1,3},{3,1},{4,6},{6,4},{5,7},{7,5},{8,10},{10,8},{9,1... | collective-permute-start | bytes 172040 | tf_op jit(solution)/shard_map/ppermute | solution.py:533
  26.5 3.6 %collective-permute-done.10.across = bf16[224,128]{1,0:T(8,128)(2,1)S(1)} collective-permute-done((bf16[224,128]{1,0:T(8,128)(2,1)S(1)}, bf16[224,128]{1,0:T(8,128)(2,1)S(1)}, u32[]{:S(2)}, u32[]{:S(2)}) %collective-permute-start.10) | collective-permute-done | bytes 57376 | tf_op jit(solution)/shard_map/ppermute | solution.py:533
  30.2 0.4 %collective-permute-done.11.far = bf16[352,128]{1,0:T(8,128)(2,1)S(1)} collective-permute-done((bf16[352,128]{1,0:T(8,128)(2,1)S(1)}, bf16[352,128]{1,0:T(8,128)(2,1)S(1)}, u32[]{:S(2)}, u32[]{:S(2)}) %collective-permute-start.11) | collective-permute-done | bytes 90144 | tf_op jit(solution)/shard_map/ppermute | solution.py:529
  30.6 1.1 %last.1 = (bf16[6,4,32,128]{3,2,1,0:T(8,128)(2,1)}, bf16[6,4,32,128]{3,2,1,0:T(8,128)(2,1)}, f32[3,3,64,72]{3,2,1,0:T(8,128)}, f32[3,64,72]{2,1,0:T(8,128)}) custom-call(f32[6,4,32,128]{3,2,1,0:T(8,128)S(1)} %get-tuple-element.54.own, f32[6,4,32,128]{3,2,1,0:T(8,128)S(1)} %get-tuple-element.55.ig_own, bf16[224,128]{1,0:T(8,128)(2,1)S(1)} %add.15.half_0, ...), custom_call_target="tpu_custom_call" | custom-call | tf_op jit(solution)/shard_map/last/pallas_call | solution.py:534
  (7 shorter events, 0.1 us)
Async XLA Ops:
  0.6 7.7 %copy-start = (bf16[6,4,64,128]{3,2,1,0:T(8,128)(2,1)S(1)}, bf16[6,4,64,128]{3,2,1,0:T(8,128)(2,1)}, u32[]{:S(2)}) copy-start(bf16[6,4,64,128]{3,2,1,0:T(8,128)(2,1)} %x.1) | copy-start | bytes 1179652
  0.6 7.7 %copy-start.1 = (bf16[6,4,64,128]{3,2,1,0:T(8,128)(2,1)S(1)}, bf16[6,4,64,128]{3,2,1,0:T(8,128)(2,1)}, u32[]{:S(2)}) copy-start(bf16[6,4,64,128]{3,2,1,0:T(8,128)(2,1)} %u.1) | copy-start | bytes 1179652
  0.7 7.7 %copy-start.2 = (bf16[3,3,64,72]{3,2,1,0:T(8,128)(2,1)S(1)}, bf16[3,3,64,72]{3,2,1,0:T(8,128)(2,1)}, u32[]{:S(2)}) copy-start(bf16[3,3,64,72]{3,2,1,0:T(8,128)(2,1)} %refs_4_.1) | copy-start | bytes 248836
  0.7 7.7 %copy-start.3 = (bf16[3,72,64]{1,2,0:T(8,128)(2,1)S(1)}, bf16[3,72,64]{1,2,0:T(8,128)(2,1)}, u32[]{:S(2)}) copy-start(bf16[3,72,64]{1,2,0:T(8,128)(2,1)} %param.6) | copy-start | bytes 82948
  2.3 8.9 %collective-permute-start.1 = (bf16[4,64,128]{2,1,0:T(8,128)(2,1)}, bf16[4,64,128]{2,1,0:T(8,128)(2,1)S(1)}, u32[]{:S(2)}, u32[]{:S(2)}) collective-permute-start(bf16[4,64,128]{2,1,0:T(8,128)(2,1)} %get-tuple-element.41), channel_id=1, source_target_pairs={{0,13},{1,4},{4,1},{5,8},{8,5},{9,12},{12,9},{13,0},{2,15},{3,6},{... | collective-permute-start | bytes 196616 | tf_op jit(solution)/shard_map/ppermute | solution.py:432
  6.8 4.3 %collective-permute-start = (bf16[3,64,128]{2,1,0:T(8,128)(2,1)}, bf16[3,64,128]{2,1,0:T(8,128)(2,1)S(1)}, u32[]{:S(2)}, u32[]{:S(2)}) collective-permute-start(bf16[3,64,128]{2,1,0:T(8,128)(2,1)} %get-tuple-element.40), channel_id=1, source_target_pairs={{0,2},{2,0},{1,3},{3,1},{4,6},{6,4},{5,7},{7,5},{8,10},{10,8},{9,1... | collective-permute-start | bytes 147464 | tf_op jit(solution)/shard_map/ppermute | solution.py:435
  11.1 1.4 %collective-permute-start.2 = (bf16[7,64,128]{2,1,0:T(8,128)(2,1)S(1)}, bf16[7,64,128]{2,1,0:T(8,128)(2,1)S(1)}, u32[]{:S(2)}, u32[]{:S(2)}) collective-permute-start(bf16[7,64,128]{2,1,0:T(8,128)(2,1)S(1)} %pad_maximum_fusion), channel_id=1, source_target_pairs={{0,1},{1,0},{2,3},{3,2},{4,5},{5,4},{6,7},{7,6},{8,9},{9,8},{10,11... | collective-permute-start | bytes 344072 | tf_op jit(solution)/shard_map/ppermute | solution.py:466
  11.2 4.2 %collective-permute-start.3 = (bf16[3,3,64,72]{3,2,1,0:T(8,128)(2,1)S(1)}, bf16[3,3,64,72]{3,2,1,0:T(8,128)(2,1)S(1)}, u32[]{:S(2)}, u32[]{:S(2)}) collective-permute-start(bf16[3,3,64,72]{3,2,1,0:T(8,128)(2,1)S(1)} %copy-done.2), channel_id=1, source_target_pairs={{0,1},{1,0},{2,3},{3,2},{4,5},{5,4},{6,7},{7,6},{8,9},{9,8},{10,11... | collective-permute-start | bytes 248840 | tf_op jit(solution)/shard_map/ppermute | solution.py:438
  11.7 3.7 %collective-permute-start.4 = (bf16[3,64,72]{2,1,0:T(8,128)(2,1)S(1)}, bf16[3,64,72]{2,1,0:T(8,128)(2,1)S(1)}, u32[]{:S(2)}, u32[]{:S(2)}) collective-permute-start(bf16[3,64,72]{2,1,0:T(8,128)(2,1)S(1)} %bitcast.6), channel_id=1, source_target_pairs={{0,1},{1,0},{2,3},{3,2},{4,5},{5,4},{6,7},{7,6},{8,9},{9,8},{10,11... | collective-permute-start | bytes 82952 | tf_op jit(solution)/shard_map/ppermute | solution.py:433
  13.8 4.2 %collective-permute-start.7 = (bf16[224,128]{1,0:T(8,128)(2,1)S(1)}, bf16[224,128]{1,0:T(8,128)(2,1)S(1)}, u32[]{:S(2)}, u32[]{:S(2)}) collective-permute-start(bf16[224,128]{1,0:T(8,128)(2,1)S(1)} %get-tuple-element.61), channel_id=1, source_target_pairs={{0,2},{2,0},{1,3},{3,1},{4,6},{6,4},{5,7},{7,5},{8,10},{10,8},{9,1... | collective-permute-start | bytes 172040 | tf_op jit(solution)/shard_map/ppermute | solution.py:489
  15.4 4.2 %collective-permute-start.5 = (bf16[224,128]{1,0:T(8,128)(2,1)S(1)}, bf16[224,128]{1,0:T(8,128)(2,1)S(1)}, u32[]{:S(2)}, u32[]{:S(2)}) collective-permute-start(bf16[224,128]{1,0:T(8,128)(2,1)S(1)} %get-tuple-element.56), channel_id=1, source_target_pairs={{0,4},{4,0},{8,12},{12,8},{1,5},{5,1},{9,13},{13,9},{2,6},{6,2},{1... | collective-permute-start | bytes 172040 | tf_op jit(solution)/shard_map/ppermute | solution.py:488
  19.6 4.6 %collective-permute-start.8 = (bf16[352,128]{1,0:T(8,128)(2,1)S(1)}, bf16[352,128]{1,0:T(8,128)(2,1)S(1)}, u32[]{:S(2)}, u32[]{:S(2)}) collective-permute-start(bf16[352,128]{1,0:T(8,128)(2,1)S(1)} %pad_maximum_fusion.1), channel_id=1, source_target_pairs={{0,4},{4,0},{8,12},{12,8},{1,5},{5,1},{9,13},{13,9},{2,6},{6,2},{1... | collective-permute-start | bytes 270344 | tf_op jit(solution)/shard_map/ppermute | solution.py:527
  19.7 6.2 %collective-permute-start.6 = (bf16[224,128]{1,0:T(8,128)(2,1)S(1)}, bf16[224,128]{1,0:T(8,128)(2,1)S(1)}, u32[]{:S(2)}, u32[]{:S(2)}) collective-permute-start(bf16[224,128]{1,0:T(8,128)(2,1)S(1)} %add.12), channel_id=1, source_target_pairs={{0,8},{4,12},{8,0},{12,4},{1,9},{5,13},{9,1},{13,5},{2,10},{6,14},... | collective-permute-start | bytes 172040 | tf_op jit(solution)/shard_map/ppermute | solution.py:525
  21.7 4.2 %collective-permute-start.9 = (bf16[6,32,128]{2,1,0:T(8,128)(2,1)S(1)}, bf16[6,32,128]{2,1,0:T(8,128)(2,1)S(1)}, u32[]{:S(2)}, u32[]{:S(2)}) collective-permute-start(bf16[6,32,128]{2,1,0:T(8,128)(2,1)S(1)} %get-tuple-element.63), channel_id=1, source_target_pairs={{0,2},{2,0},{1,3},{3,1},{4,6},{6,4},{5,7},{7,5},{8,10},{10,8},{9,1... | collective-permute-start | bytes 147464 | tf_op jit(solution)/shard_map/ppermute | solution.py:530
  24.2 6.4 %collective-permute-start.11 = (bf16[352,128]{1,0:T(8,128)(2,1)S(1)}, bf16[352,128]{1,0:T(8,128)(2,1)S(1)}, u32[]{:S(2)}, u32[]{:S(2)}) collective-permute-start(bf16[352,128]{1,0:T(8,128)(2,1)S(1)} %pad_maximum_fusion.2), channel_id=1, source_target_pairs={{0,12},{4,8},{8,4},{12,0},{1,13},{5,9},{9,5},{13,1},{2,14},{6,10},... | collective-permute-start | bytes 270344 | tf_op jit(solution)/shard_map/ppermute | solution.py:529
  25.9 4.2 %collective-permute-start.10 = (bf16[224,128]{1,0:T(8,128)(2,1)S(1)}, bf16[224,128]{1,0:T(8,128)(2,1)S(1)}, u32[]{:S(2)}, u32[]{:S(2)}) collective-permute-start(bf16[224,128]{1,0:T(8,128)(2,1)S(1)} %add.15.half_0), channel_id=1, source_target_pairs={{0,2},{2,0},{1,3},{3,1},{4,6},{6,4},{5,7},{7,5},{8,10},{10,8},{9,1... | collective-permute-start | bytes 172040 | tf_op jit(solution)/shard_map/ppermute | solution.py:533

commit v3 on v2

--- a/solution.py
+++ b/solution.py
@@ -252,7 +252,7 @@
 def fields_kernel(dims, fast, *refs):
     frames, rows, channels, width, mid, own_c, rank_count, axial_count, group = dims
     hid_in, grad_in, hid_other, grad_other, sw, tw, sw_other, tw_other = refs[:8]
-    out, out_a, out_b, ig, ig_a, ig_b, twt, wg, ig_acc, out_edges = refs[8:]
+    out, out_a, out_b, ig_acc, ig_a, ig_b, twt, wg, out_edges = refs[8:]
     own = pl.ds(pl.multiple_of(lax.axis_index("chan") * own_c, own_c), own_c)
     blank = jnp.zeros((own_c, padded(mid) - mid), F32)
 
@@ -306,8 +306,6 @@
     for f in range(frames):
         ig_a[f] = ig_acc[f, high].astype(BF16)
         ig_b[f] = ig_acc[f, rows + 1].astype(BF16)
-        for h in range(rows):
-            ig[f, h] = ig_acc[f, h + 1]
 
 
 def rest_kernel(dims, fast, *refs):
@@ -341,7 +339,7 @@
             if f == frames - 1:
                 total = total + from_hi(h).astype(F32)
             out[f, h] = total.astype(BF16)
-            total = ig_own[f, h]
+            total = ig_own[f, h + 1]
             if h == 0:
                 total = total + ig_from_lo(f).astype(F32) * has_lo
             if h == rows - 1:
@@ -493,7 +491,7 @@
     out_own, out_a, out_b, ig_own, ig_a, ig_b = call(
         functools.partial(rest_kernel, dims, fast),
         "field_products",
-        [sds(own_shape, F32), out_edge, out_edge, sds(own_shape, F32), ig_edge, ig_edge],
+        [sds(own_shape, F32), out_edge, out_edge, sds((frames, rows + 2, own_c, width), F32), ig_edge, ig_edge],
         8,
         16,
         forms
@@ -502,7 +500,6 @@
             pltpu.VMEM(cells, BF16),
             pltpu.VMEM((3 * own_c, 2 * padded(mid)), BF16),
             pltpu.VMEM((9 * own_c, 2 * padded(mid)), BF16),
-            pltpu.VMEM((frames, rows + 2, own_c, width), F32),
             pltpu.VMEM((2, rows, own_c, width), BF16),
         ],
         flops=1 << 31,

time: 31.8 us -> 31.8 us (level)
  no operation moved by 1% of the time
where the time goes in v3:
time: 31.8 us; the launch traced here: 31.6 us
  starting transfers between devices  13.2 us (42%)
  waiting for transfers between devices  10.3 us (32%)
  Pallas kernels  7.27 us (23%)
  between operations  0.74 us (2%)
    ppermute x1, starting transfers between devices, shards(): frame = lax.ppermute(frame, ('tm', 'chan'), facing(tm_count))  4.55 us
    ppermute x1, waiting for transfers between devices, shards(): across = lax.ppermute(half_0, 'axial', ring(2, 1))  3.63 us
    pallas_call x1, Pallas kernels, shards(): call(functools.partial(rest_kernel, dims, fast), 'field_products', [sds(o...  2.1 us
    ppermute x1, starting transfers between devices, shards(): apart = lax.ppermute(half_0, 'tm', pairs(4, 2))  2.05 us
    ppermute x1, waiting for transfers between devices, shards(): lax.ppermute(jnp.concatenate([half_1, out_a.reshape(-1, width)], 0), 'tm'...  1.9 us
    ppermute x1, starting transfers between devices, shards(): lax.ppermute(jnp.concatenate([half_1, out_b.reshape(-1, width)], 0), 'tm'...  1.7 us
    pallas_call x1, Pallas kernels, shards(): call(functools.partial(stage_kernel, split), 'stage', [sds((edge_count, c...  1.59 us
    ppermute x1, starting transfers between devices, shards(): got_1 = lax.ppermute(half_1, 'axial', ring(2, 1))  1.56 us
  transfers between devices with their start and end apart: 12, of which 7 were waited for; matrix products, arithmetic and copies ran while one was open for 0% of the time, Pallas kernels for 15%

profile of v3, /device:TPU:0, one launch (start us, length us, event | category | flops | bytes accessed | tf_op | source)
XLA Modules:
  0.0 31.6 jit_solution(4472400788309397973)
XLA Ops:
  0.6 0.0 copy-start
  0.6 0.0 copy-start.1
  0.7 0.0 copy-start.2
  0.7 0.0 copy-start.3
  0.7 1.6 %stage.1 = (bf16[3,64,128]{2,1,0:T(8,128)(2,1)}, bf16[4,64,128]{2,1,0:T(8,128)(2,1)}) custom-call(bf16[6,4,64,128]{3,2,1,0:T(8,128)(2,1)} %x.1, bf16[6,4,64,128]{3,2,1,0:T(8,128)(2,1)} %u.1, bf16[3,3,64,72]{3,2,1,0:T(8,128)(2,1)} %refs_4_.1, bf16[3,64,72]{2,1,0:T(8,128)(2,1)} %bitcast.4), custom_call_target="tpu_custom_call" | custom-call | tf_op jit(solution)/shard_map/stage/pallas_call | solution.py:421
  2.3 4.6 %collective-permute-start.1 = (bf16[4,64,128]{2,1,0:T(8,128)(2,1)}, bf16[4,64,128]{2,1,0:T(8,128)(2,1)S(1)}, u32[]{:S(2)}, u32[]{:S(2)}) collective-permute-start(bf16[4,64,128]{2,1,0:T(8,128)(2,1)} %get-tuple-element.41), channel_id=1, source_target_pairs={{0,13},{1,4},{4,1},{5,8},{8,5},{9,12},{12,9},{13,0},{2,15},{3,6},{... | collective-permute-start | bytes 196616 | tf_op jit(solution)/shard_map/ppermute | solution.py:430
  6.8 1.5 %collective-permute-start = (bf16[3,64,128]{2,1,0:T(8,128)(2,1)}, bf16[3,64,128]{2,1,0:T(8,128)(2,1)S(1)}, u32[]{:S(2)}, u32[]{:S(2)}) collective-permute-start(bf16[3,64,128]{2,1,0:T(8,128)(2,1)} %get-tuple-element.40), channel_id=1, source_target_pairs={{0,2},{2,0},{1,3},{3,1},{4,6},{6,4},{5,7},{7,5},{8,10},{10,8},{9,1... | collective-permute-start | bytes 147464 | tf_op jit(solution)/shard_map/ppermute | solution.py:433
  8.3 0.0 copy-done
  8.3 0.0 copy-done.1
  8.3 0.0 copy-done.2
  8.3 0.0 copy-done.3
  8.3 1.2 %inner_cells.1 = (bf16[3,4,80,128]{3,2,1,0:T(8,128)(2,1)S(1)}, bf16[3,4,80,128]{3,2,1,0:T(8,128)(2,1)S(1)}, f32[192,288]{1,0:T(8,128)S(1)}, bf16[6,6,64,128]{3,2...) custom-call(bf16[6,4,64,128]{3,2,1,0:T(8,128)(2,1)S(1)} %copy-done, ...), custom_call_target="tpu_custom_call" | custom-call | flops 2147483648 | bytes 1048576 | tf_op jit(solution)/shard_map/inner_cells/pallas_call | solution.py:446
  9.6 1.5 %collective-permute-done.refs_5_ = bf16[3,64,128]{2,1,0:T(8,128)(2,1)S(1)} collective-permute-done((bf16[3,64,128]{2,1,0:T(8,128)(2,1)}, bf16[3,64,128]{2,1,0:T(8,128)(2,1)S(1)}, u32[]{:S(2)}, u32[]{:S(2)}) %collective-permute-start) | collective-permute-done | bytes 49184 | tf_op jit(solution)/shard_map/ppermute | solution.py:433
  11.1 0.0 collective-permute-done.1.refs_6_
  11.1 0.1 collective-permute-start.2
  11.2 0.5 %collective-permute-start.3 = (bf16[3,3,64,72]{3,2,1,0:T(8,128)(2,1)S(1)}, bf16[3,3,64,72]{3,2,1,0:T(8,128)(2,1)S(1)}, u32[]{:S(2)}, u32[]{:S(2)}) collective-permute-start(bf16[3,3,64,72]{3,2,1,0:T(8,128)(2,1)S(1)} %copy-done.2), channel_id=1, source_target_pairs={{0,1},{1,0},{2,3},{3,2},{4,5},{5,4},{6,7},{7,6},{8,9},{9,8},{10,11... | collective-permute-start | bytes 248840 | tf_op jit(solution)/shard_map/ppermute | solution.py:436
  11.7 0.1 collective-permute-start.4
  11.8 0.7 %collective-permute-done.2.refs_7_ = bf16[7,64,128]{2,1,0:T(8,128)(2,1)S(1)} collective-permute-done((bf16[7,64,128]{2,1,0:T(8,128)(2,1)S(1)}, bf16[7,64,128]{2,1,0:T(8,128)(2,1)S(1)}, u32[]{:S(2)}, u32[]{:S(2)}) %collective-permute-start.2) | collective-permute-done | bytes 114720 | tf_op jit(solution)/shard_map/ppermute | solution.py:464
  12.5 1.3 %weight_grads.1 = (bf16[4,6,80,128]{3,2,1,0:T(8,128)(2,1)S(1)}, bf16[4,6,80,128]{3,2,1,0:T(8,128)(2,1)S(1)}, bf16[6,6,64,128]{3,2,1,0:T(8,128)(2,1)S(1)}, bf16[8...) custom-call(bf16[3,4,80,128]{3,2,1,0:T(8,128)(2,1)S(1)} %get-tuple-element.38.refs_0_, ...), custom_call_target="tpu_custom_call" | custom-call | tf_op jit(solution)/shard_map/weight_grads/pallas_call | solution.py:465
  13.8 1.6 %collective-permute-start.7 = (bf16[224,128]{1,0:T(8,128)(2,1)S(1)}, bf16[224,128]{1,0:T(8,128)(2,1)S(1)}, u32[]{:S(2)}, u32[]{:S(2)}) collective-permute-start(bf16[224,128]{1,0:T(8,128)(2,1)S(1)} %get-tuple-element.61), channel_id=1, source_target_pairs={{0,2},{2,0},{1,3},{3,1},{4,6},{6,4},{5,7},{7,5},{8,10},{10,8},{9,1... | collective-permute-start | bytes 172040 | tf_op jit(solution)/shard_map/ppermute | solution.py:487
  15.4 0.0 collective-permute-start.5
  15.4 0.0 collective-permute-done.4.refs_7_
  15.4 0.0 collective-permute-done.3.refs_6_
  15.4 2.1 %field_products.1 = (f32[6,4,32,128]{3,2,1,0:T(8,128)S(1)}, bf16[4,32,128]{2,1,0:T(8,128)(2,1)S(1)}, bf16[4,32,128]{2,1,0:T(8,128)(2,1)S(1)}, f32[6,6,32,128]{3,...) custom-call(bf16[4,6,80,128]{3,2,1,0:T(8,128)(2,1)S(1)} %get-tuple-element.50.refs_0_, ...), custom_call_target="tpu_custom_call" | custom-call | flops 2147483648 | bytes 1048576 | tf_op jit(solution)/shard_map/field_products/pallas_call | solution.py:491
  17.5 0.6 %collective-permute-done.7 = bf16[224,128]{1,0:T(8,128)(2,1)S(1)} collective-permute-done((bf16[224,128]{1,0:T(8,128)(2,1)S(1)}, bf16[224,128]{1,0:T(8,128)(2,1)S(1)}, u32[]{:S(2)}, u32[]{:S(2)}) %collective-permute-start.7) | collective-permute-done | bytes 57376 | tf_op jit(solution)/shard_map/ppermute | solution.py:487
  18.1 1.5 %collective-permute-done.5 = bf16[224,128]{1,0:T(8,128)(2,1)S(1)} collective-permute-done((bf16[224,128]{1,0:T(8,128)(2,1)S(1)}, bf16[224,128]{1,0:T(8,128)(2,1)S(1)}, u32[]{:S(2)}, u32[]{:S(2)}) %collective-permute-start.5) | collective-permute-done | bytes 57376 | tf_op jit(solution)/shard_map/ppermute | solution.py:486
  19.6 0.1 collective-permute-start.8
  19.7 2.0 %collective-permute-start.6 = (bf16[224,128]{1,0:T(8,128)(2,1)S(1)}, bf16[224,128]{1,0:T(8,128)(2,1)S(1)}, u32[]{:S(2)}, u32[]{:S(2)}) collective-permute-start(bf16[224,128]{1,0:T(8,128)(2,1)S(1)} %add.12), channel_id=1, source_target_pairs={{0,8},{4,12},{8,0},{12,4},{1,9},{5,13},{9,1},{13,5},{2,10},{6,14},... | collective-permute-start | bytes 172040 | tf_op jit(solution)/shard_map/ppermute | solution.py:522
  21.7 0.5 %collective-permute-start.9 = (bf16[6,32,128]{2,1,0:T(8,128)(2,1)S(1)}, bf16[6,32,128]{2,1,0:T(8,128)(2,1)S(1)}, u32[]{:S(2)}, u32[]{:S(2)}) collective-permute-start(bf16[6,32,128]{2,1,0:T(8,128)(2,1)S(1)} %get-tuple-element.63), channel_id=1, source_target_pairs={{0,2},{2,0},{1,3},{3,1},{4,6},{6,4},{5,7},{7,5},{8,10},{10,8},{9,1... | collective-permute-start | bytes 147464 | tf_op jit(solution)/shard_map/ppermute | solution.py:527
  22.3 1.9 %collective-permute-done.8.near = bf16[352,128]{1,0:T(8,128)(2,1)S(1)} collective-permute-done((bf16[352,128]{1,0:T(8,128)(2,1)S(1)}, bf16[352,128]{1,0:T(8,128)(2,1)S(1)}, u32[]{:S(2)}, u32[]{:S(2)}) %collective-permute-start.8) | collective-permute-done | bytes 90144 | tf_op jit(solution)/shard_map/ppermute | solution.py:524
  24.2 1.7 %collective-permute-start.11 = (bf16[352,128]{1,0:T(8,128)(2,1)S(1)}, bf16[352,128]{1,0:T(8,128)(2,1)S(1)}, u32[]{:S(2)}, u32[]{:S(2)}) collective-permute-start(bf16[352,128]{1,0:T(8,128)(2,1)S(1)} %pad_maximum_fusion.2), channel_id=1, source_target_pairs={{0,12},{4,8},{8,4},{12,0},{1,13},{5,9},{9,5},{13,1},{2,14},{6,10},... | collective-permute-start | bytes 270344 | tf_op jit(solution)/shard_map/ppermute | solution.py:526
  25.9 0.0 collective-permute-done.9.ig_edge
  25.9 0.0 collective-permute-done.6
  25.9 0.6 %collective-permute-start.10 = (bf16[224,128]{1,0:T(8,128)(2,1)S(1)}, bf16[224,128]{1,0:T(8,128)(2,1)S(1)}, u32[]{:S(2)}, u32[]{:S(2)}) collective-permute-start(bf16[224,128]{1,0:T(8,128)(2,1)S(1)} %add.15.half_0), channel_id=1, source_target_pairs={{0,2},{2,0},{1,3},{3,1},{4,6},{6,4},{5,7},{7,5},{8,10},{10,8},{9,1... | collective-permute-start | bytes 172040 | tf_op jit(solution)/shard_map/ppermute | solution.py:530
  26.5 3.6 %collective-permute-done.10.across = bf16[224,128]{1,0:T(8,128)(2,1)S(1)} collective-permute-done((bf16[224,128]{1,0:T(8,128)(2,1)S(1)}, bf16[224,128]{1,0:T(8,128)(2,1)S(1)}, u32[]{:S(2)}, u32[]{:S(2)}) %collective-permute-start.10) | collective-permute-done | bytes 57376 | tf_op jit(solution)/shard_map/ppermute | solution.py:530
  30.2 0.4 %collective-permute-done.11.far = bf16[352,128]{1,0:T(8,128)(2,1)S(1)} collective-permute-done((bf16[352,128]{1,0:T(8,128)(2,1)S(1)}, bf16[352,128]{1,0:T(8,128)(2,1)S(1)}, u32[]{:S(2)}, u32[]{:S(2)}) %collective-permute-start.11) | collective-permute-done | bytes 90144 | tf_op jit(solution)/shard_map/ppermute | solution.py:526
  30.6 1.1 %last.1 = (bf16[6,4,32,128]{3,2,1,0:T(8,128)(2,1)}, bf16[6,4,32,128]{3,2,1,0:T(8,128)(2,1)}, f32[3,3,64,72]{3,2,1,0:T(8,128)}, f32[3,64,72]{2,1,0:T(8,128)}) custom-call(f32[6,4,32,128]{3,2,1,0:T(8,128)S(1)} %get-tuple-element.54.own, f32[6,6,32,128]{3,2,1,0:T(8,128)S(1)} %get-tuple-element.55.ig_own, bf16[224,128]{1,0:T(8,128)(2,1)S(1)} %add.15.half_0, ...), custom_call_target="tpu_custom_call" | custom-call | tf_op jit(solution)/shard_map/last/pallas_call | solution.py:531
  (7 shorter events, 0.1 us)
Async XLA Ops:
  0.6 7.7 %copy-start = (bf16[6,4,64,128]{3,2,1,0:T(8,128)(2,1)S(1)}, bf16[6,4,64,128]{3,2,1,0:T(8,128)(2,1)}, u32[]{:S(2)}) copy-start(bf16[6,4,64,128]{3,2,1,0:T(8,128)(2,1)} %x.1) | copy-start | bytes 1179652
  0.6 7.7 %copy-start.1 = (bf16[6,4,64,128]{3,2,1,0:T(8,128)(2,1)S(1)}, bf16[6,4,64,128]{3,2,1,0:T(8,128)(2,1)}, u32[]{:S(2)}) copy-start(bf16[6,4,64,128]{3,2,1,0:T(8,128)(2,1)} %u.1) | copy-start | bytes 1179652
  0.7 7.7 %copy-start.2 = (bf16[3,3,64,72]{3,2,1,0:T(8,128)(2,1)S(1)}, bf16[3,3,64,72]{3,2,1,0:T(8,128)(2,1)}, u32[]{:S(2)}) copy-start(bf16[3,3,64,72]{3,2,1,0:T(8,128)(2,1)} %refs_4_.1) | copy-start | bytes 248836
  0.7 7.7 %copy-start.3 = (bf16[3,72,64]{1,2,0:T(8,128)(2,1)S(1)}, bf16[3,72,64]{1,2,0:T(8,128)(2,1)}, u32[]{:S(2)}) copy-start(bf16[3,72,64]{1,2,0:T(8,128)(2,1)} %param.6) | copy-start | bytes 82948
  2.3 8.9 %collective-permute-start.1 = (bf16[4,64,128]{2,1,0:T(8,128)(2,1)}, bf16[4,64,128]{2,1,0:T(8,128)(2,1)S(1)}, u32[]{:S(2)}, u32[]{:S(2)}) collective-permute-start(bf16[4,64,128]{2,1,0:T(8,128)(2,1)} %get-tuple-element.41), channel_id=1, source_target_pairs={{0,13},{1,4},{4,1},{5,8},{8,5},{9,12},{12,9},{13,0},{2,15},{3,6},{... | collective-permute-start | bytes 196616 | tf_op jit(solution)/shard_map/ppermute | solution.py:430
  6.8 4.3 %collective-permute-start = (bf16[3,64,128]{2,1,0:T(8,128)(2,1)}, bf16[3,64,128]{2,1,0:T(8,128)(2,1)S(1)}, u32[]{:S(2)}, u32[]{:S(2)}) collective-permute-start(bf16[3,64,128]{2,1,0:T(8,128)(2,1)} %get-tuple-element.40), channel_id=1, source_target_pairs={{0,2},{2,0},{1,3},{3,1},{4,6},{6,4},{5,7},{7,5},{8,10},{10,8},{9,1... | collective-permute-start | bytes 147464 | tf_op jit(solution)/shard_map/ppermute | solution.py:433
  11.1 1.4 %collective-permute-start.2 = (bf16[7,64,128]{2,1,0:T(8,128)(2,1)S(1)}, bf16[7,64,128]{2,1,0:T(8,128)(2,1)S(1)}, u32[]{:S(2)}, u32[]{:S(2)}) collective-permute-start(bf16[7,64,128]{2,1,0:T(8,128)(2,1)S(1)} %pad_maximum_fusion), channel_id=1, source_target_pairs={{0,1},{1,0},{2,3},{3,2},{4,5},{5,4},{6,7},{7,6},{8,9},{9,8},{10,11... | collective-permute-start | bytes 344072 | tf_op jit(solution)/shard_map/ppermute | solution.py:464
  11.2 4.2 %collective-permute-start.3 = (bf16[3,3,64,72]{3,2,1,0:T(8,128)(2,1)S(1)}, bf16[3,3,64,72]{3,2,1,0:T(8,128)(2,1)S(1)}, u32[]{:S(2)}, u32[]{:S(2)}) collective-permute-start(bf16[3,3,64,72]{3,2,1,0:T(8,128)(2,1)S(1)} %copy-done.2), channel_id=1, source_target_pairs={{0,1},{1,0},{2,3},{3,2},{4,5},{5,4},{6,7},{7,6},{8,9},{9,8},{10,11... | collective-permute-start | bytes 248840 | tf_op jit(solution)/shard_map/ppermute | solution.py:436
  11.7 3.7 %collective-permute-start.4 = (bf16[3,64,72]{2,1,0:T(8,128)(2,1)S(1)}, bf16[3,64,72]{2,1,0:T(8,128)(2,1)S(1)}, u32[]{:S(2)}, u32[]{:S(2)}) collective-permute-start(bf16[3,64,72]{2,1,0:T(8,128)(2,1)S(1)} %bitcast.6), channel_id=1, source_target_pairs={{0,1},{1,0},{2,3},{3,2},{4,5},{5,4},{6,7},{7,6},{8,9},{9,8},{10,11... | collective-permute-start | bytes 82952 | tf_op jit(solution)/shard_map/ppermute | solution.py:431
  13.8 4.2 %collective-permute-start.7 = (bf16[224,128]{1,0:T(8,128)(2,1)S(1)}, bf16[224,128]{1,0:T(8,128)(2,1)S(1)}, u32[]{:S(2)}, u32[]{:S(2)}) collective-permute-start(bf16[224,128]{1,0:T(8,128)(2,1)S(1)} %get-tuple-element.61), channel_id=1, source_target_pairs={{0,2},{2,0},{1,3},{3,1},{4,6},{6,4},{5,7},{7,5},{8,10},{10,8},{9,1... | collective-permute-start | bytes 172040 | tf_op jit(solution)/shard_map/ppermute | solution.py:487
  15.4 4.2 %collective-permute-start.5 = (bf16[224,128]{1,0:T(8,128)(2,1)S(1)}, bf16[224,128]{1,0:T(8,128)(2,1)S(1)}, u32[]{:S(2)}, u32[]{:S(2)}) collective-permute-start(bf16[224,128]{1,0:T(8,128)(2,1)S(1)} %get-tuple-element.56), channel_id=1, source_target_pairs={{0,4},{4,0},{8,12},{12,8},{1,5},{5,1},{9,13},{13,9},{2,6},{6,2},{1... | collective-permute-start | bytes 172040 | tf_op jit(solution)/shard_map/ppermute | solution.py:486
  19.6 4.6 %collective-permute-start.8 = (bf16[352,128]{1,0:T(8,128)(2,1)S(1)}, bf16[352,128]{1,0:T(8,128)(2,1)S(1)}, u32[]{:S(2)}, u32[]{:S(2)}) collective-permute-start(bf16[352,128]{1,0:T(8,128)(2,1)S(1)} %pad_maximum_fusion.1), channel_id=1, source_target_pairs={{0,4},{4,0},{8,12},{12,8},{1,5},{5,1},{9,13},{13,9},{2,6},{6,2},{1... | collective-permute-start | bytes 270344 | tf_op jit(solution)/shard_map/ppermute | solution.py:524
  19.7 6.2 %collective-permute-start.6 = (bf16[224,128]{1,0:T(8,128)(2,1)S(1)}, bf16[224,128]{1,0:T(8,128)(2,1)S(1)}, u32[]{:S(2)}, u32[]{:S(2)}) collective-permute-start(bf16[224,128]{1,0:T(8,128)(2,1)S(1)} %add.12), channel_id=1, source_target_pairs={{0,8},{4,12},{8,0},{12,4},{1,9},{5,13},{9,1},{13,5},{2,10},{6,14},... | collective-permute-start | bytes 172040 | tf_op jit(solution)/shard_map/ppermute | solution.py:522
  21.7 4.2 %collective-permute-start.9 = (bf16[6,32,128]{2,1,0:T(8,128)(2,1)S(1)}, bf16[6,32,128]{2,1,0:T(8,128)(2,1)S(1)}, u32[]{:S(2)}, u32[]{:S(2)}) collective-permute-start(bf16[6,32,128]{2,1,0:T(8,128)(2,1)S(1)} %get-tuple-element.63), channel_id=1, source_target_pairs={{0,2},{2,0},{1,3},{3,1},{4,6},{6,4},{5,7},{7,5},{8,10},{10,8},{9,1... | collective-permute-start | bytes 147464 | tf_op jit(solution)/shard_map/ppermute | solution.py:527
  24.2 6.4 %collective-permute-start.11 = (bf16[352,128]{1,0:T(8,128)(2,1)S(1)}, bf16[352,128]{1,0:T(8,128)(2,1)S(1)}, u32[]{:S(2)}, u32[]{:S(2)}) collective-permute-start(bf16[352,128]{1,0:T(8,128)(2,1)S(1)} %pad_maximum_fusion.2), channel_id=1, source_target_pairs={{0,12},{4,8},{8,4},{12,0},{1,13},{5,9},{9,5},{13,1},{2,14},{6,10},... | collective-permute-start | bytes 270344 | tf_op jit(solution)/shard_map/ppermute | solution.py:526
  25.9 4.2 %collective-permute-start.10 = (bf16[224,128]{1,0:T(8,128)(2,1)S(1)}, bf16[224,128]{1,0:T(8,128)(2,1)S(1)}, u32[]{:S(2)}, u32[]{:S(2)}) collective-permute-start(bf16[224,128]{1,0:T(8,128)(2,1)S(1)} %add.15.half_0), channel_id=1, source_target_pairs={{0,2},{2,0},{1,3},{3,1},{4,6},{6,4},{5,7},{7,5},{8,10},{10,8},{9,1... | collective-permute-start | bytes 172040 | tf_op jit(solution)/shard_map/ppermute | solution.py:530
